TPU v7x, 32 devices: a whole 2x2x4 slice. The times are simulated.
32 devices in a mesh: dp: 4 (over y, x), expert: 8 (over z, core).
Axes of the slice: x: 2, y: 2, z: 4, core: 2. Of those that a mesh axis runs over, the one named last changes fastest.
Arguments:
- hidden_in: bfloat16 [4096, 2880], P(('dp', 'expert')), may hold values from -6 to 6
- queries: bfloat16 [4096, 4096], P(('dp', 'expert')), may hold values from -50 to 50
- kv_pages: bfloat16 [512, 128, 1024], P(('dp', 'expert')), may hold values from -4.5 to 4.5
- page_table: int32 [128, 4], P(('dp', 'expert')), may hold values from 0 to 15, as said below
- new_rows: int32 [128], P(('dp', 'expert')), may hold values from 1 to 125, as said below
- context: int32 [128], P(('dp', 'expert')), may hold values from 1 to 512, as said below
- sink_logits: float32 [64], replicated, may hold values from 0 to 8
- out_proj: bfloat16 [4096, 2880], P('dp'), may hold values from -0.09375 to 0.09375
- norm_gain: float32 [2880], replicated, may hold values from 0.1 to 1.9
- routes: int32 [4096, 4], P(('dp', 'expert')), may hold values from 0 to 31, all different within a row; in each aligned block of 128 rows (0 to 127, 128 to 255, ...) at most 20 rows name the same one
- route_weights: float32 [4096, 4], P(('dp', 'expert')), may hold values from 0.05 to 1
- gate_up: bfloat16 [32, 2, 2880, 2048], P('expert', None, None, 'dp'), may hold values from -0.109375 to 0.109375
- down_proj: bfloat16 [32, 2048, 2880], P('expert', 'dp'), may hold values from -0.125 to 0.125
Outputs:
- layer_out: bfloat16 [4096, 2880], P(('dp', 'expert'))
Inputs may be any that keep to these rules, and one draw needn't show every extreme that they name: `page_table`: each request's table row lists distinct pages of its own block of 16 pages; each block's table holds each of its page numbers once. The new_rows of one block of 4 requests sum to 128; one to three requests of each block have more than one. new_rows <= context; in every block some request has context 4 * 128. Within the 128 rows of one block, no expert is named by more than 20 routes; some expert reaches 20 in every draw.
All inputs are finite; a program needn't handle non-finite values.
Results may differ from a plain program's by a relative error of at most 0.015.
Values may be sent and summed in bfloat16 or wider, within the bound.
No kernel may reach another device: no remote copies, remote signals or barrier semaphores. Data moves between devices by JAX's collectives and lax.ppermute only.
A program may use at most 128 MiB of HBM per device.

v0:
```python
import functools

import jax
import jax.numpy as jnp
from jax import lax
from jax.experimental import pallas as pl
from jax.experimental.pallas import tpu as pltpu
from jax.sharding import Mesh
from jax.sharding import PartitionSpec as P

QH = 64
KVH = 8
HD = 64
E = 32
CAP = 20
TOP = 4
TERMS = 3
BACK = (2, 3, 0, 1)
GROUP = QH // KVH
TILE = 32
VMEM_MIB = 58

norm_eps = 1e-05
F32 = jnp.float32
BF16 = jnp.bfloat16


def params(mib, **kw):
    return pltpu.CompilerParams(vmem_limit_bytes=mib << 20, **kw)


def attend_kernel(
    col_s, rows_s, ctx_s, table_s, sink_s, q_ref, kv_ref, *refs, kv_heads, reqs, per_req
):
    o_ref = refs[-1]
    page_len = kv_ref.shape[1]
    span = per_req * page_len
    width = 2 * HD
    lane = lax.broadcasted_iota(jnp.int32, (1, width), 1)
    low = lane < HD
    slot = lax.broadcasted_iota(jnp.int32, (1, span), 1)
    row_in = lax.broadcasted_iota(jnp.int32, (TILE, 1), 0)
    head0 = col_s[0] * kv_heads * GROUP

    def one_tile(req, first, last, tile):
        r0 = pl.multiple_of(tile * TILE, TILE)
        row = row_in + r0
        mine = (row >= first) & (row < last)
        limit = jnp.where(mine, row + (ctx_s[req] - last), -1)
        limit = jnp.concatenate([limit] * GROUP, axis=0)
        seen = slot <= limit
        for k in range(kv_heads):
            kv = jnp.concatenate(
                [
                    kv_ref[table_s[req * per_req + p], :, k * width : (k + 1) * width]
                    for p in range(per_req)
                ],
                axis=0,
            )
            parts, sinks = [], []
            for g in range(0, GROUP, 2):
                c0 = (k * GROUP + g) * HD
                pair = q_ref[pl.ds(r0, TILE), c0 : c0 + width].astype(F32) * (HD**-0.5)
                parts.append(jnp.where(low, pair, 0.0).astype(BF16))
                parts.append(jnp.where(low, pltpu.roll(pair, HD, 1), 0.0).astype(BF16))
                for h in (g, g + 1):
                    sinks.append(jnp.full((TILE, 1), sink_s[head0 + k * GROUP + h], F32))
            q = jnp.concatenate(parts, axis=0)
            sink = jnp.concatenate(sinks, axis=0)
            score = lax.dot_general(q, kv, (((1,), (1,)), ((), ())), preferred_element_type=F32)
            score = jnp.where(seen, score, -jnp.inf)
            top = jnp.maximum(jnp.max(score, axis=1, keepdims=True), sink)
            prob = jnp.exp(score - top).astype(BF16)
            ones_v = jnp.where(low, jnp.ones_like(kv), kv)
            both = jnp.dot(prob, ones_v, preferred_element_type=F32)
            swapped = pltpu.roll(both, HD, 1)
            norm = jnp.where(low, both, swapped) + jnp.exp(sink - top)
            out = jnp.where(low, swapped, both) / norm
            for g in range(0, GROUP, 2):
                a = out[g * TILE : (g + 1) * TILE]
                b = out[(g + 1) * TILE : (g + 2) * TILE]
                c0 = (k * GROUP + g) * HD
                old = o_ref[pl.ds(r0, TILE), c0 : c0 + width]
                new = jnp.where(low, a, b).astype(BF16)
                o_ref[pl.ds(r0, TILE), c0 : c0 + width] = jnp.where(mine, new, old)

    def one_req(req, first):
        last = first + rows_s[req]

        def step(tile, carry):
            one_tile(req, first, last, tile)
            return carry

        lax.fori_loop(first // TILE, (last - 1) // TILE + 1, step, 0)
        return last

    lax.fori_loop(0, reqs, one_req, jnp.int32(0))


def attend_group(
    col, queries, kv_pages, page_table, new_rows, context, sink_logits, groups, before=()
):
    rows = queries.shape[0]
    pages, page_len, kv_width = kv_pages.shape
    reqs, per_req = page_table.shape
    kv_heads = KVH // groups
    q_width = queries.shape[1] // groups
    body = functools.partial(attend_kernel, kv_heads=kv_heads, reqs=reqs, per_req=per_req)
    flops = 2 * 2 * rows * q_width * per_req * page_len
    return pl.pallas_call(
        body,
        grid_spec=pltpu.PrefetchScalarGridSpec(
            num_scalar_prefetch=5,
            grid=(1,),
            in_specs=[
                pl.BlockSpec((rows, q_width), lambda i, col, *_: (0, col[0])),
                pl.BlockSpec(
                    (pages, page_len, kv_width // groups), lambda i, col, *_: (0, 0, col[0])
                ),
                *[pl.BlockSpec(memory_space=pl.ANY)] * len(before),
            ],
            out_specs=pl.BlockSpec((rows, q_width), lambda i, *_: (0, 0)),
        ),
        out_shape=jax.ShapeDtypeStruct((rows, q_width), BF16),
        compiler_params=params(VMEM_MIB),
        cost_estimate=pl.CostEstimate(
            flops=8 * flops,
            bytes_accessed=2 * (2 * rows * q_width + pages * page_len * kv_width // groups),
            transcendentals=0,
        ),
        name="attend",
    )(col, new_rows, context, page_table.reshape(-1), sink_logits, queries, kv_pages, *before)


def mix_kernel(x_ref, a_ref, b_ref, c_ref, d_ref, gain_ref, info_ref, mixed_ref, normed_ref):
    total = a_ref[...].astype(F32) + b_ref[...].astype(F32)
    total = total + c_ref[...].astype(F32) + d_ref[...].astype(F32)
    mixed = (x_ref[...].astype(F32) + total).astype(BF16)
    mixed_ref[...] = mixed
    m = mixed.astype(F32)
    scale = lax.rsqrt(jnp.mean(m * m, axis=0, keepdims=True) + norm_eps)
    normed = (jnp.transpose(m * scale) * gain_ref[...]).astype(BF16)
    rows, width = normed.shape
    normed_ref[:, :width] = normed
    fill = normed_ref.shape[1] - width
    if fill:
        lane = lax.broadcasted_iota(jnp.int32, (rows, 128), 1) - (128 - fill)
        rest = info_ref[...]
        info = rest.astype(BF16).astype(F32)
        for i in range(1, TERMS):
            rest = rest - rest.astype(BF16).astype(F32)
            moved = pltpu.roll(rest.astype(BF16).astype(F32), i * TOP, 1)
            info = jnp.where((lane >= (i + 1) * TOP) & (lane < (i + 2) * TOP), moved, info)
        normed_ref[:, width:] = info[:, 128 - fill :].astype(BF16)


def mix_and_norm(hidden_t, terms_t, norm_gain, routes, route_weights):
    width, rows = hidden_t.shape
    fill = -width % 128
    info = jnp.concatenate([routes.astype(F32), route_weights], axis=1)
    info = jnp.pad(info, ((0, 0), (128 - fill, fill - info.shape[1]))) if fill else jnp.zeros((rows, 128))
    normed = jax.ShapeDtypeStruct((rows, -(-width // 128) * 128), BF16)
    return pl.pallas_call(
        mix_kernel,
        out_shape=[jax.ShapeDtypeStruct((width, rows), BF16), normed],
        compiler_params=params(VMEM_MIB),
        name="mix_norm",
    )(hidden_t, *terms_t, norm_gain.reshape(1, width), info)


def finish_kernel(mixed_ref, *refs):
    parts, out_ref = refs[:-1], refs[-1]
    total = parts[0][...].astype(F32)
    for part in parts[1:]:
        total = total + part[...].astype(F32)
    total = jnp.transpose(total)[: mixed_ref.shape[0]]
    out_ref[...] = (mixed_ref[...].astype(F32) + total).astype(BF16)


def finish(mixed_t, parts):
    return pl.pallas_call(
        finish_kernel,
        out_shape=jax.ShapeDtypeStruct(mixed_t.shape, BF16),
        compiler_params=params(VMEM_MIB),
        name="finish",
    )(mixed_t, *parts)


def pick_kernel(bases_s, *refs, count, local, width):
    pieces, (x_ref, far_ref, hot_ref) = refs[:count], refs[-3:]
    each, wide = pieces[0].shape
    slots = count * CAP
    both = 2 * local
    at = width - (wide - 128)
    upper = (
        lax.broadcasted_iota(jnp.int32, (each, each), 0)
        <= lax.broadcasted_iota(jnp.int32, (each, each), 1)
    ).astype(F32).astype(BF16)
    members = []
    for s in range(count):
        info = jnp.transpose(pieces[s][:, wide - 128 :].astype(F32))[at : at + TOP]
        for e in range(both):
            expert = (bases_s[e // local] + e % local).astype(F32)
            members.append(jnp.max(jnp.where(info == expert, 1.0, 0.0), axis=0, keepdims=True))
    member = jnp.concatenate(members, axis=0)
    counts = jnp.dot(member.astype(BF16), upper, preferred_element_type=F32)
    rank = jnp.where(member > 0.0, counts - 1.0, -100.0)
    place = lax.broadcasted_iota(jnp.int32, (slots, each), 0).astype(F32)
    columns = []
    for s in range(count):
        want = place - float(s * CAP)
        hots = [
            jnp.where(want == rank[s * both + e : s * both + e + 1], 1.0, 0.0) for e in range(both)
        ]
        columns.append(jnp.concatenate(hots, axis=0).astype(BF16))
    hot = jnp.concatenate(columns, axis=1)
    rows = jnp.concatenate([ref[...] for ref in pieces], axis=0)
    half = local * slots
    for i, ref in enumerate((x_ref, far_ref)):
        picked = jnp.dot(hot[i * half : (i + 1) * half], rows, preferred_element_type=F32)
        ref[...] = picked.astype(BF16).reshape(ref.shape)
    rank_t = jnp.transpose(rank).astype(BF16)
    slot = lax.broadcasted_iota(jnp.int32, (count * both, both * slots), 1)
    line = lax.broadcasted_iota(jnp.int32, (count * both, both * slots), 0)
    for i, s in enumerate(BACK):
        first = (line - s * both) * slots
        owner = (slot >= first) & (slot < first + slots) & (line >= s * both)
        owner = owner & (line < (s + 1) * both)
        owner = jnp.where(owner, 1.0, 0.0)
        want = slot[:1] - s * CAP - jnp.sum(
            jnp.where(owner > 0.0, line - s * both, 0), axis=0, keepdims=True
        ) * slots
        held = jnp.dot(rank_t, owner.astype(BF16), preferred_element_type=F32)
        hot_ref[i * each : (i + 1) * each, :] = jnp.where(held == want.astype(F32), 1.0, 0.0).astype(
            BF16
        )


def pick_rows(bases, pieces, local, width, before=(), later=()):
    count = len(pieces)
    each, wide = pieces[0].shape
    slots = count * CAP
    smem = pl.BlockSpec(memory_space=pltpu.SMEM)
    vmem = pl.BlockSpec(memory_space=pltpu.VMEM)
    hand_on = pl.BlockSpec(memory_space=pl.ANY)
    x = jax.ShapeDtypeStruct((local, slots, wide), BF16)
    return pl.pallas_call(
        functools.partial(pick_kernel, count=count, local=local, width=width),
        in_specs=[smem] + [vmem] * count + [hand_on] * (len(before) + len(later)),
        out_specs=[hand_on] * len(later) + [vmem] * 3,
        out_shape=[jax.ShapeDtypeStruct(p.shape, p.dtype) for p in later]
        + [x, x, jax.ShapeDtypeStruct((count * each, 2 * local * slots), BF16)],
        input_output_aliases={1 + count + len(before) + i: i for i in range(len(later))},
        compiler_params=params(VMEM_MIB),
        cost_estimate=pl.CostEstimate(
            flops=2 * 4 * local * slots * count * each * wide,
            bytes_accessed=2 * (count * each + 2 * local * slots) * wide,
            transcendentals=0,
        ),
        name="pick",
    )(bases, *pieces, *before, *later)


def expert_kernel(bases_s, *refs, groups):
    xs, (up_ref, down_ref) = refs[:groups], refs[groups : groups + 2]
    ys, acc_ref = refs[-1 - groups : -1], refs[-1]
    part_at = pl.program_id(1)
    width = down_ref.shape[1]
    wide = xs[0].shape[2]
    x = jnp.concatenate([ref[0] for ref in xs], axis=0)
    gate = jnp.dot(x[:, :width], up_ref[0, 0], preferred_element_type=F32)
    up = jnp.dot(x[:, :width], up_ref[0, 1], preferred_element_type=F32)
    act = ((up + 1.0) * gate * jax.nn.sigmoid(1.702 * gate)).astype(BF16)
    part = lax.dot_general(
        act, down_ref[0], (((1,), (1,)), ((), ())), preferred_element_type=F32
    )

    @pl.when(part_at == 0)
    def _():
        acc_ref[...] = part

    @pl.when(part_at == pl.num_programs(1) - 1)
    def _():
        info = x[:, wide - 128 :].astype(F32)
        lane = lax.broadcasted_iota(jnp.int32, info.shape, 1) - (width - (wide - 128))
        share = 0.0
        for i in range(TERMS):
            share = share + pltpu.roll(info, 128 - (i + 1) * TOP, 1)
        expert = (bases_s[0] + pl.program_id(0)).astype(F32)
        mine = (lane >= 0) & (lane < TOP) & (info == expert)
        share = jnp.sum(jnp.where(mine, share, 0.0), axis=1, keepdims=True)
        slots = xs[0].shape[1]
        for i, y_ref in enumerate(ys):
            at = slice(i * slots, (i + 1) * slots)
            y_ref[0, :, :width] = ((acc_ref[at] + part[at]) * share[at]).astype(BF16)
            if wide > width:
                y_ref[0, :, width:] = jnp.zeros((slots, wide - width), BF16)


def run_experts(bases, xs, gate_up, down_t, before=(), later=()):
    groups = len(xs)
    local, slots, wide = xs[0].shape
    width, units = gate_up.shape[2:]
    splits = 2
    unit = units // splits
    x_spec = pl.BlockSpec((1, slots, wide), lambda e, i: (e, 0, 0))
    hand_on = pl.BlockSpec(memory_space=pl.ANY)
    return pl.pallas_call(
        functools.partial(expert_kernel, groups=groups),
        grid=(local, splits),
        in_specs=[
            pl.BlockSpec(memory_space=pltpu.SMEM),
            *[x_spec] * groups,
            pl.BlockSpec((1, 2, width, unit), lambda e, i: (e, 0, 0, i)),
            pl.BlockSpec((1, width, unit), lambda e, i: (e, 0, i)),
            *[hand_on] * (len(before) + len(later)),
        ],
        out_specs=[hand_on] * len(later) + [x_spec] * groups,
        out_shape=[jax.ShapeDtypeStruct(p.shape, p.dtype) for p in later]
        + [jax.ShapeDtypeStruct((local, slots, wide), BF16)] * groups,
        input_output_aliases={3 + groups + len(before) + i: i for i in range(len(later))},
        scratch_shapes=[pltpu.VMEM((groups * slots, width), F32)],
        compiler_params=params(VMEM_MIB),
        cost_estimate=pl.CostEstimate(
            flops=2 * 2 * 3 * groups * local * slots * width * units,
            bytes_accessed=2 * (gate_up.size + down_t.size + 2 * groups * xs[0].size),
            transcendentals=0,
        ),
        name="experts",
    )(bases, *xs, gate_up, down_t, *before, *later)


def spread_kernel(hot_ref, mine_ref, far_ref, *refs):
    leave_ref, keep_ref = refs[-2:]
    local, slots, wide = mine_ref.shape
    y = [ref[...].reshape(local * slots, wide) for ref in (mine_ref, far_ref)]
    y = jnp.concatenate(y, axis=0)
    half = leave_ref.shape[0]
    for i, ref in enumerate((leave_ref, keep_ref)):
        hot = hot_ref[i * half : (i + 1) * half, :]
        ref[...] = jnp.dot(hot, y, preferred_element_type=F32).astype(BF16)


def spread_rows(hot, mine, far, before=()):
    rows = hot.shape[0]
    wide = mine.shape[2]
    vmem = pl.BlockSpec(memory_space=pltpu.VMEM)
    return pl.pallas_call(
        spread_kernel,
        in_specs=[vmem] * 3 + [pl.BlockSpec(memory_space=pl.ANY)] * len(before),
        out_specs=[vmem] * 2,
        out_shape=[jax.ShapeDtypeStruct((rows // 2, wide), BF16)] * 2,
        compiler_params=params(VMEM_MIB),
        cost_estimate=pl.CostEstimate(
            flops=4 * hot.size * wide,
            bytes_accessed=2 * (2 * mine.size + rows * wide),
            transcendentals=0,
        ),
        name="spread",
    )(hot, mine, far, *before)


def exchange(value, axes, count, step):
    return lax.ppermute(value, axes, [(i, i ^ step) for i in range(count)])


def add(*terms):
    total = terms[0].astype(F32)
    for term in terms[1:]:
        total = total + term.astype(F32)
    return total.astype(BF16)


def attention_and_norm(
    hidden_in, queries, kv_pages, page_table, new_rows, context, sink_logits, out_proj, norm_gain,
    routes, route_weights, dp, dp_count,
):
    me = lax.axis_index(dp)

    def attend(step, before=()):
        col = (me ^ step).astype(jnp.int32).reshape(1)
        part = attend_group(
            col, queries, kv_pages, page_table, new_rows, context, sink_logits, dp_count, before
        )
        return exchange(part, dp, dp_count, step) if step else part

    def project(part):
        term = jnp.dot(part, out_proj, preferred_element_type=F32).astype(BF16)
        return jnp.swapaxes(term, 0, 1)

    order = list(range(dp_count - 1, 0, -1)) + [0]
    parts, terms, back = [], [], []
    for at, step in enumerate(order):
        before = list(terms[-1:]) if at > 1 else []
        parts.append(attend(step, before))
        if at:
            terms.append(project(parts[at - 1]))
            back.append(exchange(terms[-1], dp, dp_count, order[at - 1]))
    terms = back + [project(parts[-1])]
    hidden_t = jnp.swapaxes(hidden_in, 0, 1)
    return mix_and_norm(hidden_t, terms, norm_gain, routes, route_weights)


def layer_gathered(
    hidden_in, queries, kv_pages, page_table, new_rows, context, sink_logits, out_proj, norm_gain,
    routes, route_weights, gate_up, down_proj, *, sizes,
):
    ny, nx, nz, nc = sizes
    local, _, width, _ = gate_up.shape
    core = lax.axis_index("core")
    bases = (lax.axis_index("z") * nc + jnp.stack([core, core ^ 1])) * local
    bases = bases.astype(jnp.int32)
    everyone = ("y", "x", "z", "core")
    per_y, per_x = nx * nz * nc, nz * nc
    hops = {"first": (per_x, per_y), "second": (per_y, per_x)}

    def to(value, axis, step=1):
        if axis in hops:
            pairs = [(i, i ^ hops[axis][i % nc]) for i in range(ny * nx * nz * nc)]
            return lax.ppermute(value, everyone, pairs)
        return exchange(value, axis, nz if axis == "z" else nc, step)

    mixed, normed = attention_and_norm(
        hidden_in, queries, kv_pages, page_table, new_rows, context, sink_logits, out_proj,
        norm_gain, routes, route_weights, ("y", "x"), ny * nx,
    )
    each = normed.shape[0]
    down_t = jnp.swapaxes(down_proj, 1, 2)
    rows = {0: normed, 1: to(normed, "z", 1), 2: to(normed, "z", 2)}
    pairs = ((0, 2), (3, 1))
    near, sums, cames = {}, [], []
    for pair in pairs:
        xs, hots = [], []
        for r in pair:
            if r not in near:
                near[r] = (to(rows[r], "first"), to(rows[r], "second"))
            plane = [rows[r], *near[r], to(near[r][0], "second")]
            if r == 0:
                later = [rows[1], rows[2]]
                rows[1], rows[2], x, far, hot = pick_rows(bases, plane, local, width, (), later)
                rows[3] = to(rows[2], "z", 1)
                near[1] = (to(rows[1], "first"), to(rows[1], "second"))
            elif r == 2:
                rows[3], x, far, hot = pick_rows(bases, plane, local, width, (), [rows[3]])
                near[3] = (to(rows[3], "first"), to(rows[3], "second"))
            else:
                x, far, hot = pick_rows(bases, plane, local, width)
            xs += [x, to(far, "core")]
            hots.append(hot)
        if pair == pairs[0]:
            ys = run_experts(bases, xs, gate_up, down_t)
        else:
            ys = run_experts(bases, xs, gate_up, down_t, before=cames)
        for at, r in enumerate(pair):
            y, far = ys[2 * at], to(ys[2 * at + 1], "core")
            leave, keep = spread_rows(hots[at], y, far)
            came = to(leave, "second")
            cames.append(came)
            last = to(add(keep[each:], came[each:]), "first")
            total = add(keep[:each], came[:each], last)
            sums.append(to(total, "z", r) if r else total)
    return jnp.swapaxes(finish(mixed, sums), 0, 1)


def layer_sent(
    hidden_in, queries, kv_pages, page_table, new_rows, context, sink_logits, out_proj, norm_gain,
    routes, route_weights, gate_up, down_proj, *, dp_count,
):
    row_count, model_width = hidden_in.shape
    mixed, normed = attention_and_norm(
        hidden_in, queries, kv_pages, page_table, new_rows, context, sink_logits, out_proj,
        norm_gain, routes, route_weights, "dp", dp_count,
    )
    mixed = jnp.swapaxes(mixed, 0, 1)
    normed = normed[:, :model_width]
    assign = routes.reshape(-1)
    onehot = (assign[:, None] == jnp.arange(E, dtype=jnp.int32)[None, :]).astype(jnp.int32)
    slot_index = jnp.sum((jnp.cumsum(onehot, axis=0) - onehot) * onehot, axis=1)
    source = jnp.arange(assign.shape[0], dtype=jnp.int32) // routes.shape[1]
    send_rows = jnp.zeros((E, CAP, model_width), BF16).at[assign, slot_index].set(normed[source])
    copies = jnp.broadcast_to(send_rows[None], (dp_count,) + send_rows.shape)
    copies = copies.reshape(dp_count * E, CAP, model_width)
    everyone = ("dp", "expert")
    blocks = lax.all_to_all(copies, everyone, split_axis=0, concat_axis=0, tiled=True)
    local = gate_up.shape[0]
    shape = blocks.shape
    blocks = blocks.reshape(shape[0] // local, local, CAP, model_width)
    gate_up_f = jnp.einsum("sjcd,jtdf->sjctf", blocks, gate_up, preferred_element_type=F32)
    gate, up = gate_up_f[:, :, :, 0, :], gate_up_f[:, :, :, 1, :]
    hidden = ((up + 1.0) * gate * jax.nn.sigmoid(1.702 * gate)).astype(BF16)
    partials = jnp.einsum("sjcf,jfd->sjcd", hidden, down_proj, preferred_element_type=F32)
    partials = partials.astype(BF16).reshape(shape)
    back = lax.all_to_all(partials, everyone, split_axis=0, concat_axis=0, tiled=True)
    back = jnp.sum(back.reshape(dp_count, E, CAP, model_width).astype(F32), axis=0)
    picked = back[assign, slot_index] * route_weights.reshape(-1)[:, None]
    mix = jnp.sum(picked.reshape(row_count, routes.shape[1], model_width), axis=1)
    return (mixed.astype(F32) + mix).astype(BF16)


def solution(mesh):
    dp_count, expert_count = mesh.shape["dp"], mesh.shape["expert"]
    if dp_count == 4 and expert_count == 8:
        sizes = (2, 2, 4, 2)
        grid = Mesh(mesh.devices.reshape(sizes), ("y", "x", "z", "core"))
        dp, expert, body = ("y", "x"), ("z", "core"), functools.partial(layer_gathered, sizes=sizes)
    else:
        grid = mesh
        dp, expert, body = ("dp",), ("expert",), functools.partial(layer_sent, dp_count=dp_count)
    everyone = dp + expert
    return jax.shard_map(
        body,
        mesh=grid,
        in_specs=(
            P(everyone, None),
            P(everyone, None),
            P(everyone, None, None),
            P(everyone, None),
            P(everyone),
            P(everyone),
            P(),
            P(dp, None),
            P(),
            P(everyone, None),
            P(everyone, None),
            P(expert, None, None, dp),
            P(expert, dp, None),
        ),
        out_specs=P(everyone, None),
        check_vma=False,
    )
```

profile of v0, /device:TPU:13, one launch (start us, length us, event | category | flops | bytes accessed | tf_op | source)
XLA Modules:
  0.0 455.9 jit_solution(11824459795146924692)
XLA Ops:
  1.3 10.8 %attend.4 = bf16[128,1024]{1,0:T(8,128)(2,1)} custom-call(s32[1]{0:T(128)} %bitcast.1.col_s, s32[4]{0:T(128)} %rows_s.7, s32[4]{0:T(128)} %ctx_s.7, s32[16]{0:T(128)} %reshape.22.table_s, f32[64]{0:T(128)} %sink_s.7, bf16[128,4096]{1,0:T(8,128)(2,1)} %q_ref.7, bf16[16,128,1024]{2,1,0:T(8,128)(2,1)} %kv_ref.7), custom_call_target="tpu_custom_call" | custom-call | flops 2147483648 | bytes 1572864 | tf_op jit(solution)/shard_map/attend/pallas_call | solution.py:110
  12.1 10.9 %attend.5 = bf16[128,1024]{1,0:T(8,128)(2,1)} custom-call(s32[1]{0:T(128)} %bitcast.3.col_s, s32[4]{0:T(128)} %rows_s.7, s32[4]{0:T(128)} %ctx_s.7, s32[16]{0:T(128)} %reshape.22.table_s, f32[64]{0:T(128)} %sink_s.7, bf16[128,4096]{1,0:T(8,128)(2,1)} %q_ref.7, bf16[16,128,1024]{2,1,0:T(8,128)(2,1)} %kv_ref.7), custom_call_target="tpu_custom_call" | custom-call | flops 2147483648 | bytes 1572864 | tf_op jit(solution)/shard_map/attend/pallas_call | solution.py:110
  23.1 2.4 collective-permute-start.2
  25.5 5.5 %fusion.refs_0_ = bf16[2880,128]{1,0:T(8,128)(2,1)} fusion(bf16[128,1024]{1,0:T(8,128)(2,1)} %collective-permute-done, bf16[1024,2880]{0,1:T(8,128)(2,1)} %param.20), kind=kOutput, calls=%fused_computation.4 | convolution fusion | flops 755343360 | bytes 6897664 | tf_op jit(solution)/shard_map/dot_general | solution.py:388
  31.1 10.8 %attend.6 = bf16[128,1024]{1,0:T(8,128)(2,1)} custom-call(s32[1]{0:T(128)} %bitcast.5.col_s, s32[4]{0:T(128)} %rows_s.7, s32[4]{0:T(128)} %ctx_s.7, s32[16]{0:T(128)} %reshape.22.table_s, f32[64]{0:T(128)} %sink_s.7, bf16[128,4096]{1,0:T(8,128)(2,1)} %q_ref.7, bf16[16,128,1024]{2,1,0:T(8,128)(2,1)} %kv_ref.7, bf16[2880,128]{1,0:T(8,128)(2,1)} %fusion.refs_0_), custom_call_target="tpu_custom_call" | custom-call | flops 2147483648 | bytes 1572864 | tf_op jit(solution)/shard_map/attend/pallas_call | solution.py:110
  43.0 2.6 fusion.1.refs_0_
  45.8 7.3 %collective-permute-done.4 = bf16[128,1024]{1,0:T(8,128)(2,1)S(1)} collective-permute-done((bf16[128,1024]{1,0:T(8,128)(2,1)}, bf16[128,1024]{1,0:T(8,128)(2,1)S(1)}, u32[]{:S(2)}, u32[]{:S(2)}) %collective-permute-start.4) | collective-permute-done | bytes 262176 | tf_op jit(solution)/shard_map/ppermute | solution.py:364
  53.1 2.6 fusion.2
  57.8 10.8 %attend.7 = bf16[128,1024]{1,0:T(8,128)(2,1)} custom-call(s32[1]{0:T(128)} %bitcast.7.col_s, s32[4]{0:T(128)} %rows_s.7, s32[4]{0:T(128)} %ctx_s.7, s32[16]{0:T(128)} %reshape.22.table_s, f32[64]{0:T(128)} %sink_s.7, bf16[128,4096]{1,0:T(8,128)(2,1)} %q_ref.7, bf16[16,128,1024]{2,1,0:T(8,128)(2,1)} %kv_ref.7, bf16[2880,128]{1,0:T(8,128)(2,1)} %fusion.1.refs_0_), custom_call_target="tpu_custom_call" | custom-call | flops 2147483648 | bytes 1572864 | tf_op jit(solution)/shard_map/attend/pallas_call | solution.py:110
  68.6 5.3 %fusion.3.d_ref = bf16[2880,128]{1,0:T(8,128)(2,1)} fusion(bf16[128,1024]{1,0:T(8,128)(2,1)} %attend.7, bf16[1024,2880]{0,1:T(8,128)(2,1)} %param.20), kind=kOutput, calls=%fused_computation.7 | convolution fusion | flops 755343360 | bytes 6897664 | tf_op jit(solution)/shard_map/dot_general | solution.py:388
  74.8 4.7 %mix_norm.1 = (bf16[2880,128]{1,0:T(8,128)(2,1)}, bf16[128,2944]{1,0:T(8,128)(2,1)}) custom-call(bf16[2880,128]{1,0:T(8,128)(2,1)} %bitcast.27, bf16[2880,128]{1,0:T(8,128)(2,1)} %collective-permute-done.1.a_ref, bf16[2880,128]{1,0:T(8,128)(2,1)} %collective-permute-done.3.b_ref, bf16[2880,128]{1,0:T(8,128)(2,1)} %copy-done.11, ...), custom_call_target="tpu_custom_call" | custom-call | tf_op jit(solution)/shard_map/mix_norm/pallas_call | solution.py:163
  82.2 3.4 collective-permute-start.10
  85.6 8.9 %collective-permute-done.6.refs_1_ = bf16[128,2944]{1,0:T(8,128)(2,1)S(1)} collective-permute-done((bf16[128,2944]{1,0:T(8,128)(2,1)}, bf16[128,2944]{1,0:T(8,128)(2,1)S(1)}, u32[]{:S(2)}, u32[]{:S(2)}) %collective-permute-start.6) | collective-permute-done | bytes 753696 | tf_op jit(solution)/shard_map/ppermute | solution.py:420
  96.1 1.6 collective-permute-done.7.refs_2_
  97.7 13.9 %collective-permute-done.9.refs_4_ = bf16[128,2944]{1,0:T(8,128)(2,1)S(1)} collective-permute-done((bf16[128,2944]{1,0:T(8,128)(2,1)}, bf16[128,2944]{1,0:T(8,128)(2,1)S(1)}, u32[]{:S(2)}, u32[]{:S(2)}) %collective-permute-start.9) | collective-permute-done | bytes 753696 | tf_op jit(solution)/shard_map/ppermute | solution.py:364
  111.7 5.5 %collective-permute-done.10.refs_5_ = bf16[128,2944]{1,0:T(8,128)(2,1)S(1)} collective-permute-done((bf16[128,2944]{1,0:T(8,128)(2,1)}, bf16[128,2944]{1,0:T(8,128)(2,1)S(1)}, u32[]{:S(2)}, u32[]{:S(2)}) %collective-permute-start.10) | collective-permute-done | bytes 753696 | tf_op jit(solution)/shard_map/ppermute | solution.py:364
  118.1 5.8 %pick.4 = (bf16[128,2944]{1,0:T(8,128)(2,1)}, bf16[128,2944]{1,0:T(8,128)(2,1)}, bf16[4,80,2944]{2,1,0:T(8,128)(2,1)}, bf16[4,80,2944]{2,1,0:T(8,128)(2,1)}, bf16[512,640]{1,0:T(8,128)(2,1)}) custom-call(s32[2]{0:T(128)} %fusion.4.bases_s, bf16[128,2944]{1,0:T(8,128)(2,1)} %get-tuple-element.39.refs_0_, ...), custom_call_target="tpu_custom_call", output_to_operand_aliasing={{0}: (5, {}), {1}: (6, {})} | custom-call | flops 3858759680 | bytes 6782976 | tf_op jit(solution)/shard_map/pick/pallas_call | solution.py:247
  124.0 15.4 %collective-permute-done.12.refs_1_ = bf16[128,2944]{1,0:T(8,128)(2,1)S(1)} collective-permute-done((bf16[128,2944]{1,0:T(8,128)(2,1)}, bf16[128,2944]{1,0:T(8,128)(2,1)S(1)}, u32[]{:S(2)}, u32[]{:S(2)}) %collective-permute-start.12) | collective-permute-done | bytes 753696 | tf_op jit(solution)/shard_map/ppermute | solution.py:420
  139.4 7.5 %collective-permute-start.11 = (bf16[4,80,2944]{2,1,0:T(8,128)(2,1)}, bf16[4,80,2944]{2,1,0:T(8,128)(2,1)S(1)}, u32[]{:S(2)}, u32[]{:S(2)}) collective-permute-start(bf16[4,80,2944]{2,1,0:T(8,128)(2,1)} %get-tuple-element.42), channel_id=1, source_target_pairs={{0,1},{1,0},{2,3},{3,2},{4,5},{5,4},{6,7},{7,6},{8,9},{9,8},{10,11... | collective-permute-start | bytes 5652488 | tf_op jit(solution)/shard_map/ppermute | solution.py:364
  146.9 4.1 collective-permute-done.14.refs_3_
  151.9 5.9 %pick.5 = (bf16[128,2944]{1,0:T(8,128)(2,1)}, bf16[4,80,2944]{2,1,0:T(8,128)(2,1)}, bf16[4,80,2944]{2,1,0:T(8,128)(2,1)}, bf16[512,640]{1,0:T(8,128)(2,1)}) custom-call(s32[2]{0:T(128)} %fusion.4.bases_s, bf16[128,2944]{1,0:T(8,128)(2,1)} %get-tuple-element.43.refs_0_, bf16[128,2944]{1,0:T(8,128)(2,1)} %copy-done.30, ...), custom_call_target="tpu_custom_call", output_to_operand_aliasing={{0}: (5, {})} | custom-call | flops 3858759680 | bytes 6782976 | tf_op jit(solution)/shard_map/pick/pallas_call | solution.py:247
  157.8 5.5 %collective-permute-start.16 = (bf16[4,80,2944]{2,1,0:T(8,128)(2,1)}, bf16[4,80,2944]{2,1,0:T(8,128)(2,1)S(1)}, u32[]{:S(2)}, u32[]{:S(2)}) collective-permute-start(bf16[4,80,2944]{2,1,0:T(8,128)(2,1)} %get-tuple-element.45), channel_id=1, source_target_pairs={{0,1},{1,0},{2,3},{3,2},{4,5},{5,4},{6,7},{7,6},{8,9},{9,8},{10,11... | collective-permute-start | bytes 5652488 | tf_op jit(solution)/shard_map/ppermute | solution.py:364
  163.2 1.7 collective-permute-start.28
  165.0 1.9 collective-permute-done.16.refs_3_
  168.2 24.7 %experts.2 = (bf16[4,80,2944]{2,1,0:T(8,128)(2,1)}, bf16[4,80,2944]{2,1,0:T(8,128)(2,1)}, bf16[4,80,2944]{2,1,0:T(8,128)(2,1)}, bf16[4,80,2944]{2,1,0:T(8,128)(2,1)}) custom-call(s32[2]{0:T(128)} %fusion.4.bases_s, bf16[4,80,2944]{2,1,0:T(8,128)(2,1)} %get-tuple-element.41.refs_0_, bf16[4,80,2944]{2,1,0:T(8,128)(2,1)} %copy-done.18, ...), custom_call_target="tpu_custom_call" | custom-call | flops 22649241600 | bytes 50462720 | tf_op jit(solution)/shard_map/experts/pallas_call | solution.py:308
  193.4 1.7 collective-permute-start.24
  197.2 12.1 %collective-permute-done.29.refs_2_ = bf16[128,2944]{1,0:T(8,128)(2,1)S(1)} collective-permute-done((bf16[128,2944]{1,0:T(8,128)(2,1)S(1)}, bf16[128,2944]{1,0:T(8,128)(2,1)S(1)}, u32[]{:S(2)}, u32[]{:S(2)}) %collective-permute-start.29) | collective-permute-done | bytes 753696 | tf_op jit(solution)/shard_map/ppermute | solution.py:420
  209.3 3.4 collective-permute-done.24.refs_1_
  212.7 1.6 collective-permute-start.26
  214.3 6.1 %collective-permute-done.30.refs_3_ = bf16[128,2944]{1,0:T(8,128)(2,1)} collective-permute-done((bf16[128,2944]{1,0:T(8,128)(2,1)S(1)}, bf16[128,2944]{1,0:T(8,128)(2,1)}, u32[]{:S(2)}, u32[]{:S(2)}) %collective-permute-start.30) | collective-permute-done | bytes 753696 | tf_op jit(solution)/shard_map/ppermute | solution.py:420
  220.4 5.8 %pick.7 = (bf16[4,80,2944]{2,1,0:T(8,128)(2,1)}, bf16[4,80,2944]{2,1,0:T(8,128)(2,1)}, bf16[512,640]{1,0:T(8,128)(2,1)}) custom-call(s32[2]{0:T(128)} %fusion.4.bases_s, bf16[128,2944]{1,0:T(8,128)(2,1)} %get-tuple-element.59.refs_0_, bf16[128,2944]{1,0:T(8,128)(2,1)} %copy-done.22, bf16[128,2944]{1,0:T(8,128)(2,1)} %copy-done.29, ...), custom_call_target="tpu_custom_call" | custom-call | flops 3858759680 | bytes 6782976 | tf_op jit(solution)/shard_map/pick/pallas_call | solution.py:247
  228.3 8.2 %collective-permute-done.26.refs_3_ = bf16[128,2944]{1,0:T(8,128)(2,1)} collective-permute-done((bf16[128,2944]{1,0:T(8,128)(2,1)S(1)}, bf16[128,2944]{1,0:T(8,128)(2,1)}, u32[]{:S(2)}, u32[]{:S(2)}) %collective-permute-start.26) | collective-permute-done | bytes 753696 | tf_op jit(solution)/shard_map/ppermute | solution.py:420
  236.5 5.9 %pick.6 = (bf16[4,80,2944]{2,1,0:T(8,128)(2,1)}, bf16[4,80,2944]{2,1,0:T(8,128)(2,1)}, bf16[512,640]{1,0:T(8,128)(2,1)}) custom-call(s32[2]{0:T(128)} %fusion.4.bases_s, bf16[128,2944]{1,0:T(8,128)(2,1)} %get-tuple-element.55.refs_0_, bf16[128,2944]{1,0:T(8,128)(2,1)} %copy-done.27, bf16[128,2944]{1,0:T(8,128)(2,1)} %copy-done.31, ...), custom_call_target="tpu_custom_call" | custom-call | flops 3858759680 | bytes 6782976 | tf_op jit(solution)/shard_map/pick/pallas_call | solution.py:247
  244.6 6.0 %spread.4 = (bf16[256,2944]{1,0:T(8,128)(2,1)}, bf16[256,2944]{1,0:T(8,128)(2,1)}) custom-call(bf16[512,640]{1,0:T(8,128)(2,1)} %get-tuple-element.40.hot_ref, bf16[4,80,2944]{2,1,0:T(8,128)(2,1)} %get-tuple-element.46.mine_ref, bf16[4,80,2944]{2,1,0:T(8,128)(2,1)} %copy-done.16), custom_call_target="tpu_custom_call" | custom-call | flops 3858759680 | bytes 6782976 | tf_op jit(solution)/shard_map/spread/pallas_call | solution.py:348
  252.0 6.0 %spread.5 = (bf16[256,2944]{1,0:T(8,128)(2,1)}, bf16[256,2944]{1,0:T(8,128)(2,1)}) custom-call(bf16[512,640]{1,0:T(8,128)(2,1)} %get-tuple-element.50.hot_ref, bf16[4,80,2944]{2,1,0:T(8,128)(2,1)} %get-tuple-element.51.mine_ref, bf16[4,80,2944]{2,1,0:T(8,128)(2,1)} %copy-done.15), custom_call_target="tpu_custom_call" | custom-call | flops 3858759680 | bytes 6782976 | tf_op jit(solution)/shard_map/spread/pallas_call | solution.py:348
  259.4 10.3 %collective-permute-done.18.refs_6_ = bf16[256,2944]{1,0:T(8,128)(2,1)S(1)} collective-permute-done((bf16[256,2944]{1,0:T(8,128)(2,1)}, bf16[256,2944]{1,0:T(8,128)(2,1)S(1)}, u32[]{:S(2)}, u32[]{:S(2)}) %collective-permute-start.18) | collective-permute-done | bytes 1507360 | tf_op jit(solution)/shard_map/ppermute | solution.py:420
  269.7 16.1 %collective-permute-done.21.refs_7_ = bf16[256,2944]{1,0:T(8,128)(2,1)S(1)} collective-permute-done((bf16[256,2944]{1,0:T(8,128)(2,1)}, bf16[256,2944]{1,0:T(8,128)(2,1)S(1)}, u32[]{:S(2)}, u32[]{:S(2)}) %collective-permute-start.21) | collective-permute-done | bytes 1507360 | tf_op jit(solution)/shard_map/ppermute | solution.py:420
  287.0 24.8 %experts.3 = (bf16[4,80,2944]{2,1,0:T(8,128)(2,1)}, bf16[4,80,2944]{2,1,0:T(8,128)(2,1)}, bf16[4,80,2944]{2,1,0:T(8,128)(2,1)}, bf16[4,80,2944]{2,1,0:T(8,128)(2,1)}) custom-call(s32[2]{0:T(128)} %fusion.4.bases_s, bf16[4,80,2944]{2,1,0:T(8,128)(2,1)} %get-tuple-element.57.refs_0_, bf16[4,80,2944]{2,1,0:T(8,128)(2,1)} %copy-done.17, ...), custom_call_target="tpu_custom_call" | custom-call | flops 22649241600 | bytes 50462720 | tf_op jit(solution)/shard_map/experts/pallas_call | solution.py:308
  312.8 3.6 collective-permute-done.32.far_ref
  317.6 6.0 %spread.6 = (bf16[256,2944]{1,0:T(8,128)(2,1)}, bf16[256,2944]{1,0:T(8,128)(2,1)}) custom-call(bf16[512,640]{1,0:T(8,128)(2,1)} %get-tuple-element.56.hot_ref, bf16[4,80,2944]{2,1,0:T(8,128)(2,1)} %get-tuple-element.62.mine_ref, bf16[4,80,2944]{2,1,0:T(8,128)(2,1)} %copy-done.21), custom_call_target="tpu_custom_call" | custom-call | flops 3858759680 | bytes 6782976 | tf_op jit(solution)/shard_map/spread/pallas_call | solution.py:348
  325.0 6.2 %spread.7 = (bf16[256,2944]{1,0:T(8,128)(2,1)}, bf16[256,2944]{1,0:T(8,128)(2,1)}) custom-call(bf16[512,640]{1,0:T(8,128)(2,1)} %get-tuple-element.66.hot_ref, bf16[4,80,2944]{2,1,0:T(8,128)(2,1)} %get-tuple-element.67.mine_ref, bf16[4,80,2944]{2,1,0:T(8,128)(2,1)} %copy-done.19), custom_call_target="tpu_custom_call" | custom-call | flops 3858759680 | bytes 6782976 | tf_op jit(solution)/shard_map/spread/pallas_call | solution.py:348
  334.7 13.8 %collective-permute-done.33 = bf16[256,2944]{1,0:T(8,128)(2,1)S(1)} collective-permute-done((bf16[256,2944]{1,0:T(8,128)(2,1)}, bf16[256,2944]{1,0:T(8,128)(2,1)S(1)}, u32[]{:S(2)}, u32[]{:S(2)}) %collective-permute-start.33) | collective-permute-done | bytes 1507360 | tf_op jit(solution)/shard_map/ppermute | solution.py:420
  350.1 30.6 %collective-permute-done.37 = bf16[256,2944]{1,0:T(8,128)(2,1)S(1)} collective-permute-done((bf16[256,2944]{1,0:T(8,128)(2,1)}, bf16[256,2944]{1,0:T(8,128)(2,1)S(1)}, u32[]{:S(2)}, u32[]{:S(2)}) %collective-permute-start.37) | collective-permute-done | bytes 1507360 | tf_op jit(solution)/shard_map/ppermute | solution.py:420
  382.7 2.4 collective-permute-start.23
  385.8 6.3 %collective-permute-done.38 = bf16[128,2944]{1,0:T(8,128)(2,1)S(1)} collective-permute-done((bf16[128,2944]{1,0:T(8,128)(2,1)S(1)}, bf16[128,2944]{1,0:T(8,128)(2,1)S(1)}, u32[]{:S(2)}, u32[]{:S(2)}) %collective-permute-start.38) | collective-permute-done | bytes 753696 | tf_op jit(solution)/shard_map/ppermute | solution.py:420
  395.0 37.8 %collective-permute-done.23.refs_1_ = bf16[128,2944]{1,0:T(8,128)(2,1)S(1)} collective-permute-done((bf16[128,2944]{1,0:T(8,128)(2,1)S(1)}, bf16[128,2944]{1,0:T(8,128)(2,1)S(1)}, u32[]{:S(2)}, u32[]{:S(2)}) %collective-permute-start.23) | collective-permute-done | bytes 753696 | tf_op jit(solution)/shard_map/ppermute | solution.py:364
  432.8 18.1 %collective-permute-done.35.refs_2_ = bf16[128,2944]{1,0:T(8,128)(2,1)S(1)} collective-permute-done((bf16[128,2944]{1,0:T(8,128)(2,1)S(1)}, bf16[128,2944]{1,0:T(8,128)(2,1)S(1)}, u32[]{:S(2)}, u32[]{:S(2)}) %collective-permute-start.35) | collective-permute-done | bytes 753696 | tf_op jit(solution)/shard_map/ppermute | solution.py:364
  452.1 3.4 finish.1
  (142 shorter events, 39.5 us)
Async XLA Ops:
  12.1 13.4 %collective-permute-start = (bf16[128,1024]{1,0:T(8,128)(2,1)}, bf16[128,1024]{1,0:T(8,128)(2,1)}, u32[]{:S(2)}, u32[]{:S(2)}) collective-permute-start(bf16[128,1024]{1,0:T(8,128)(2,1)} %attend.4), channel_id=1, source_target_pairs={{0,24},{8,16},{16,8},{24,0},{1,25},{9,17},{17,9},{25,1},{2,26},{10... | collective-permute-start | bytes 786440 | tf_op jit(solution)/shard_map/ppermute | solution.py:364
  12.1 30.8 %slice-start = ((s8[5898240]{0:T(1024)(128)(4,1)}), s8[1703936]{0:T(1024)(128)(4,1)S(1)}, s32[]{:S(2)}) async-start(s8[5898240]{0:T(1024)(128)(4,1)} %bitcast.25), calls=%async_computation | async-start | bytes 3407872
  23.1 19.9 %collective-permute-start.2 = (bf16[128,1024]{1,0:T(8,128)(2,1)}, bf16[128,1024]{1,0:T(8,128)(2,1)S(1)}, u32[]{:S(2)}, u32[]{:S(2)}) collective-permute-start(bf16[128,1024]{1,0:T(8,128)(2,1)} %attend.5), channel_id=1, source_target_pairs={{0,16},{8,24},{16,0},{24,8},{1,17},{9,25},{17,1},{25,9},{2,18},{10... | collective-permute-start | bytes 786440 | tf_op jit(solution)/shard_map/ppermute | solution.py:364
  30.9 43.0 %collective-permute-start.1 = (bf16[2880,128]{1,0:T(8,128)(2,1)}, bf16[2880,128]{1,0:T(8,128)(2,1)}, u32[]{:S(2)}, u32[]{:S(2)}) collective-permute-start(bf16[2880,128]{1,0:T(8,128)(2,1)} %fusion.refs_0_), channel_id=1, source_target_pairs={{0,24},{8,16},{16,8},{24,0},{1,25},{9,17},{17,9},{25,1},{2,26},{10... | collective-permute-start | bytes 2211848 | tf_op jit(solution)/shard_map/ppermute | solution.py:364
  41.9 11.2 %collective-permute-start.4 = (bf16[128,1024]{1,0:T(8,128)(2,1)}, bf16[128,1024]{1,0:T(8,128)(2,1)S(1)}, u32[]{:S(2)}, u32[]{:S(2)}) collective-permute-start(bf16[128,1024]{1,0:T(8,128)(2,1)} %attend.6), channel_id=1, source_target_pairs={{0,8},{8,0},{16,24},{24,16},{1,9},{9,1},{17,25},{25,17},{2,10},{10... | collective-permute-start | bytes 786440 | tf_op jit(solution)/shard_map/ppermute | solution.py:364
  45.5 28.4 %collective-permute-start.3 = (bf16[2880,128]{1,0:T(8,128)(2,1)}, bf16[2880,128]{1,0:T(8,128)(2,1)}, u32[]{:S(2)}, u32[]{:S(2)}) collective-permute-start(bf16[2880,128]{1,0:T(8,128)(2,1)} %fusion.1.refs_0_), channel_id=1, source_target_pairs={{0,16},{8,24},{16,0},{24,8},{1,17},{9,25},{17,1},{25,9},{2,18},{10... | collective-permute-start | bytes 2211848 | tf_op jit(solution)/shard_map/ppermute | solution.py:364
  55.7 18.3 %collective-permute-start.5 = (bf16[2880,128]{1,0:T(8,128)(2,1)}, bf16[2880,128]{1,0:T(8,128)(2,1)S(1)}, u32[]{:S(2)}, u32[]{:S(2)}) collective-permute-start(bf16[2880,128]{1,0:T(8,128)(2,1)} %fusion.2), channel_id=1, source_target_pairs={{0,8},{8,0},{16,24},{24,16},{1,9},{9,1},{17,25},{25,17},{2,10},{10... | collective-permute-start | bytes 2211848 | tf_op jit(solution)/shard_map/ppermute | solution.py:364
  79.6 15.0 %collective-permute-start.6 = (bf16[128,2944]{1,0:T(8,128)(2,1)}, bf16[128,2944]{1,0:T(8,128)(2,1)S(1)}, u32[]{:S(2)}, u32[]{:S(2)}) collective-permute-start(bf16[128,2944]{1,0:T(8,128)(2,1)} %get-tuple-element.39.refs_0_), channel_id=1, source_target_pairs={{0,8},{1,17},{2,10},{3,19},{4,12},{5,21},{6,14},{7,23},{8,0},{9,25... | collective-permute-start | bytes 2261000 | tf_op jit(solution)/shard_map/ppermute | solution.py:420
  80.5 17.2 %collective-permute-start.7 = (bf16[128,2944]{1,0:T(8,128)(2,1)}, bf16[128,2944]{1,0:T(8,128)(2,1)S(1)}, u32[]{:S(2)}, u32[]{:S(2)}) collective-permute-start(bf16[128,2944]{1,0:T(8,128)(2,1)} %get-tuple-element.39.refs_0_), channel_id=1, source_target_pairs={{0,16},{1,9},{2,18},{3,11},{4,20},{5,13},{6,22},{7,15},{8,24},{9,1... | collective-permute-start | bytes 2261000 | tf_op jit(solution)/shard_map/ppermute | solution.py:420
  80.9 30.8 %collective-permute-start.9 = (bf16[128,2944]{1,0:T(8,128)(2,1)}, bf16[128,2944]{1,0:T(8,128)(2,1)S(1)}, u32[]{:S(2)}, u32[]{:S(2)}) collective-permute-start(bf16[128,2944]{1,0:T(8,128)(2,1)} %get-tuple-element.39.refs_0_), channel_id=1, source_target_pairs={{0,2},{2,0},{4,6},{6,4},{1,3},{3,1},{5,7},{7,5},{8,10},{10,8},{12,... | collective-permute-start | bytes 2261000 | tf_op jit(solution)/shard_map/ppermute | solution.py:364
  82.2 35.0 %collective-permute-start.10 = (bf16[128,2944]{1,0:T(8,128)(2,1)}, bf16[128,2944]{1,0:T(8,128)(2,1)S(1)}, u32[]{:S(2)}, u32[]{:S(2)}) collective-permute-start(bf16[128,2944]{1,0:T(8,128)(2,1)} %get-tuple-element.39.refs_0_), channel_id=1, source_target_pairs={{0,4},{2,6},{4,0},{6,2},{1,5},{3,7},{5,1},{7,3},{8,12},{10,14},{12... | collective-permute-start | bytes 2261000 | tf_op jit(solution)/shard_map/ppermute | solution.py:364
  94.5 22.7 %copy-start.23 = (bf16[128,2944]{1,0:T(8,128)(2,1)}, bf16[128,2944]{1,0:T(8,128)(2,1)S(1)}, u32[]{:S(2)}) copy-start(bf16[128,2944]{1,0:T(8,128)(2,1)S(1)} %collective-permute-done.6.refs_1_) | copy-start | bytes 2260996
  94.5 22.7 %collective-permute-start.8 = (bf16[128,2944]{1,0:T(8,128)(2,1)S(1)}, bf16[128,2944]{1,0:T(8,128)(2,1)}, u32[]{:S(2)}, u32[]{:S(2)}) collective-permute-start(bf16[128,2944]{1,0:T(8,128)(2,1)S(1)} %collective-permute-done.6.refs_1_), channel_id=1, source_target_pairs={{0,16},{1,9},{2,18},{3,11},{4,20},{5,13},{6,22},{7,15},{8,24},{9,1... | collective-permute-start | bytes 2261000 | tf_op jit(solution)/shard_map/ppermute | solution.py:420
  97.7 19.5 %copy-start.24 = (bf16[128,2944]{1,0:T(8,128)(2,1)}, bf16[128,2944]{1,0:T(8,128)(2,1)S(1)}, u32[]{:S(2)}) copy-start(bf16[128,2944]{1,0:T(8,128)(2,1)S(1)} %collective-permute-done.7.refs_2_) | copy-start | bytes 2260996
  123.9 15.5 %collective-permute-start.12 = (bf16[128,2944]{1,0:T(8,128)(2,1)}, bf16[128,2944]{1,0:T(8,128)(2,1)S(1)}, u32[]{:S(2)}, u32[]{:S(2)}) collective-permute-start(bf16[128,2944]{1,0:T(8,128)(2,1)} %get-tuple-element.43.refs_0_), channel_id=1, source_target_pairs={{0,8},{1,17},{2,10},{3,19},{4,12},{5,21},{6,14},{7,23},{8,0},{9,25... | collective-permute-start | bytes 2261000 | tf_op jit(solution)/shard_map/ppermute | solution.py:420
  123.9 23.0 %collective-permute-start.13 = (bf16[128,2944]{1,0:T(8,128)(2,1)}, bf16[128,2944]{1,0:T(8,128)(2,1)S(1)}, u32[]{:S(2)}, u32[]{:S(2)}) collective-permute-start(bf16[128,2944]{1,0:T(8,128)(2,1)} %get-tuple-element.43.refs_0_), channel_id=1, source_target_pairs={{0,16},{1,9},{2,18},{3,11},{4,20},{5,13},{6,22},{7,15},{8,24},{9,1... | collective-permute-start | bytes 2261000 | tf_op jit(solution)/shard_map/ppermute | solution.py:420
  123.9 23.0 %collective-permute-start.15 = (bf16[128,2944]{1,0:T(8,128)(2,1)}, bf16[128,2944]{1,0:T(8,128)(2,1)S(1)}, u32[]{:S(2)}, u32[]{:S(2)}) collective-permute-start(bf16[128,2944]{1,0:T(8,128)(2,1)} %get-tuple-element.43.refs_0_), channel_id=1, source_target_pairs={{0,2},{2,0},{4,6},{6,4},{1,3},{3,1},{5,7},{7,5},{8,10},{10,8},{12,... | collective-permute-start | bytes 2261000 | tf_op jit(solution)/shard_map/ppermute | solution.py:364
  139.4 11.6 %collective-permute-start.14 = (bf16[128,2944]{1,0:T(8,128)(2,1)S(1)}, bf16[128,2944]{1,0:T(8,128)(2,1)S(1)}, u32[]{:S(2)}, u32[]{:S(2)}) collective-permute-start(bf16[128,2944]{1,0:T(8,128)(2,1)S(1)} %collective-permute-done.12.refs_1_), channel_id=1, source_target_pairs={{0,16},{1,9},{2,18},{3,11},{4,20},{5,13},{6,22},{7,15},{8,24},{9,1... | collective-permute-start | bytes 2261000 | tf_op jit(solution)/shard_map/ppermute | solution.py:420
  139.4 23.8 %copy-start.26 = (bf16[128,2944]{1,0:T(8,128)(2,1)S(1)}, bf16[128,2944]{1,0:T(8,128)(2,1)}, u32[]{:S(2)}) copy-start(bf16[128,2944]{1,0:T(8,128)(2,1)} %get-tuple-element.59.refs_0_) | copy-start | bytes 2260996
  139.4 25.6 %collective-permute-start.11 = (bf16[4,80,2944]{2,1,0:T(8,128)(2,1)}, bf16[4,80,2944]{2,1,0:T(8,128)(2,1)S(1)}, u32[]{:S(2)}, u32[]{:S(2)}) collective-permute-start(bf16[4,80,2944]{2,1,0:T(8,128)(2,1)} %get-tuple-element.42), channel_id=1, source_target_pairs={{0,1},{1,0},{2,3},{3,2},{4,5},{5,4},{6,7},{7,6},{8,9},{9,8},{10,11... | collective-permute-start | bytes 5652488 | tf_op jit(solution)/shard_map/ppermute | solution.py:364
  157.8 9.2 %collective-permute-start.16 = (bf16[4,80,2944]{2,1,0:T(8,128)(2,1)}, bf16[4,80,2944]{2,1,0:T(8,128)(2,1)S(1)}, u32[]{:S(2)}, u32[]{:S(2)}) collective-permute-start(bf16[4,80,2944]{2,1,0:T(8,128)(2,1)} %get-tuple-element.45), channel_id=1, source_target_pairs={{0,1},{1,0},{2,3},{3,2},{4,5},{5,4},{6,7},{7,6},{8,9},{9,8},{10,11... | collective-permute-start | bytes 5652488 | tf_op jit(solution)/shard_map/ppermute | solution.py:364
  163.2 32.6 %collective-permute-start.28 = (bf16[128,2944]{1,0:T(8,128)(2,1)S(1)}, bf16[128,2944]{1,0:T(8,128)(2,1)S(1)}, u32[]{:S(2)}, u32[]{:S(2)}) collective-permute-start(bf16[128,2944]{1,0:T(8,128)(2,1)S(1)} %copy-done.26), channel_id=1, source_target_pairs={{0,8},{1,17},{2,10},{3,19},{4,12},{5,21},{6,14},{7,23},{8,0},{9,25... | collective-permute-start | bytes 2261000 | tf_op jit(solution)/shard_map/ppermute | solution.py:420
  192.9 50.4 %collective-permute-start.17 = (bf16[4,80,2944]{2,1,0:T(8,128)(2,1)}, bf16[4,80,2944]{2,1,0:T(8,128)(2,1)S(1)}, u32[]{:S(2)}, u32[]{:S(2)}) collective-permute-start(bf16[4,80,2944]{2,1,0:T(8,128)(2,1)} %get-tuple-element.47), channel_id=1, source_target_pairs={{0,1},{1,0},{2,3},{3,2},{4,5},{5,4},{6,7},{7,6},{8,9},{9,8},{10,11... | collective-permute-start | bytes 5652488 | tf_op jit(solution)/shard_map/ppermute | solution.py:364
  193.3 16.0 %collective-permute-start.29 = (bf16[128,2944]{1,0:T(8,128)(2,1)S(1)}, bf16[128,2944]{1,0:T(8,128)(2,1)S(1)}, u32[]{:S(2)}, u32[]{:S(2)}) collective-permute-start(bf16[128,2944]{1,0:T(8,128)(2,1)S(1)} %copy-done.26), channel_id=1, source_target_pairs={{0,16},{1,9},{2,18},{3,11},{4,20},{5,13},{6,22},{7,15},{8,24},{9,1... | collective-permute-start | bytes 2261000 | tf_op jit(solution)/shard_map/ppermute | solution.py:420
  193.4 19.3 %collective-permute-start.24 = (bf16[128,2944]{1,0:T(8,128)(2,1)}, bf16[128,2944]{1,0:T(8,128)(2,1)S(1)}, u32[]{:S(2)}, u32[]{:S(2)}) collective-permute-start(bf16[128,2944]{1,0:T(8,128)(2,1)} %get-tuple-element.55.refs_0_), channel_id=1, source_target_pairs={{0,8},{1,17},{2,10},{3,19},{4,12},{5,21},{6,14},{7,23},{8,0},{9,25... | collective-permute-start | bytes 2261000 | tf_op jit(solution)/shard_map/ppermute | solution.py:420
  195.1 55.6 %collective-permute-start.20 = (bf16[4,80,2944]{2,1,0:T(8,128)(2,1)}, bf16[4,80,2944]{2,1,0:T(8,128)(2,1)S(1)}, u32[]{:S(2)}, u32[]{:S(2)}) collective-permute-start(bf16[4,80,2944]{2,1,0:T(8,128)(2,1)} %get-tuple-element.52), channel_id=1, source_target_pairs={{0,1},{1,0},{2,3},{3,2},{4,5},{5,4},{6,7},{7,6},{8,9},{9,8},{10,11... | collective-permute-start | bytes 5652488 | tf_op jit(solution)/shard_map/ppermute | solution.py:364
  195.8 24.5 %copy-start.22 = (bf16[128,2944]{1,0:T(8,128)(2,1)}, bf16[128,2944]{1,0:T(8,128)(2,1)S(1)}, u32[]{:S(2)}) copy-start(bf16[128,2944]{1,0:T(8,128)(2,1)S(1)} %collective-permute-done.28.refs_1_) | copy-start | bytes 2260996
  195.8 24.5 %collective-permute-start.30 = (bf16[128,2944]{1,0:T(8,128)(2,1)S(1)}, bf16[128,2944]{1,0:T(8,128)(2,1)}, u32[]{:S(2)}, u32[]{:S(2)}) collective-permute-start(bf16[128,2944]{1,0:T(8,128)(2,1)S(1)} %collective-permute-done.28.refs_1_), channel_id=1, source_target_pairs={{0,16},{1,9},{2,18},{3,11},{4,20},{5,13},{6,22},{7,15},{8,24},{9,1... | collective-permute-start | bytes 2261000 | tf_op jit(solution)/shard_map/ppermute | solution.py:420
  209.3 19.0 %collective-permute-start.25 = (bf16[128,2944]{1,0:T(8,128)(2,1)}, bf16[128,2944]{1,0:T(8,128)(2,1)S(1)}, u32[]{:S(2)}, u32[]{:S(2)}) collective-permute-start(bf16[128,2944]{1,0:T(8,128)(2,1)} %get-tuple-element.55.refs_0_), channel_id=1, source_target_pairs={{0,16},{1,9},{2,18},{3,11},{4,20},{5,13},{6,22},{7,15},{8,24},{9,1... | collective-permute-start | bytes 2261000 | tf_op jit(solution)/shard_map/ppermute | solution.py:420
  212.7 23.8 %collective-permute-start.26 = (bf16[128,2944]{1,0:T(8,128)(2,1)S(1)}, bf16[128,2944]{1,0:T(8,128)(2,1)}, u32[]{:S(2)}, u32[]{:S(2)}) collective-permute-start(bf16[128,2944]{1,0:T(8,128)(2,1)S(1)} %collective-permute-done.24.refs_1_), channel_id=1, source_target_pairs={{0,16},{1,9},{2,18},{3,11},{4,20},{5,13},{6,22},{7,15},{8,24},{9,1... | collective-permute-start | bytes 2261000 | tf_op jit(solution)/shard_map/ppermute | solution.py:420
  226.2 33.2 %collective-permute-start.31 = (bf16[4,80,2944]{2,1,0:T(8,128)(2,1)}, bf16[4,80,2944]{2,1,0:T(8,128)(2,1)}, u32[]{:S(2)}, u32[]{:S(2)}) collective-permute-start(bf16[4,80,2944]{2,1,0:T(8,128)(2,1)} %get-tuple-element.61), channel_id=1, source_target_pairs={{0,1},{1,0},{2,3},{3,2},{4,5},{5,4},{6,7},{7,6},{8,9},{9,8},{10,11... | collective-permute-start | bytes 5652488 | tf_op jit(solution)/shard_map/ppermute | solution.py:364
  242.4 17.0 %collective-permute-start.27 = (bf16[4,80,2944]{2,1,0:T(8,128)(2,1)}, bf16[4,80,2944]{2,1,0:T(8,128)(2,1)S(1)}, u32[]{:S(2)}, u32[]{:S(2)}) collective-permute-start(bf16[4,80,2944]{2,1,0:T(8,128)(2,1)} %get-tuple-element.58), channel_id=1, source_target_pairs={{0,1},{1,0},{2,3},{3,2},{4,5},{5,4},{6,7},{7,6},{8,9},{9,8},{10,11... | collective-permute-start | bytes 5652488 | tf_op jit(solution)/shard_map/ppermute | solution.py:364
  250.6 19.1 %collective-permute-start.18 = (bf16[256,2944]{1,0:T(8,128)(2,1)}, bf16[256,2944]{1,0:T(8,128)(2,1)S(1)}, u32[]{:S(2)}, u32[]{:S(2)}) collective-permute-start(bf16[256,2944]{1,0:T(8,128)(2,1)} %get-tuple-element.49), channel_id=1, source_target_pairs={{0,16},{1,9},{2,18},{3,11},{4,20},{5,13},{6,22},{7,15},{8,24},{9,1... | collective-permute-start | bytes 4521992 | tf_op jit(solution)/shard_map/ppermute | solution.py:420
  258.0 27.8 %collective-permute-start.21 = (bf16[256,2944]{1,0:T(8,128)(2,1)}, bf16[256,2944]{1,0:T(8,128)(2,1)S(1)}, u32[]{:S(2)}, u32[]{:S(2)}) collective-permute-start(bf16[256,2944]{1,0:T(8,128)(2,1)} %get-tuple-element.54), channel_id=1, source_target_pairs={{0,16},{1,9},{2,18},{3,11},{4,20},{5,13},{6,22},{7,15},{8,24},{9,1... | collective-permute-start | bytes 4521992 | tf_op jit(solution)/shard_map/ppermute | solution.py:420
  259.4 26.4 %copy-start.17 = (bf16[4,80,2944]{2,1,0:T(8,128)(2,1)}, bf16[4,80,2944]{2,1,0:T(8,128)(2,1)S(1)}, u32[]{:S(2)}) copy-start(bf16[4,80,2944]{2,1,0:T(8,128)(2,1)S(1)} %collective-permute-done.27.refs_1_) | copy-start | bytes 5652484
  311.8 4.6 %collective-permute-start.32 = (bf16[4,80,2944]{2,1,0:T(8,128)(2,1)}, bf16[4,80,2944]{2,1,0:T(8,128)(2,1)S(1)}, u32[]{:S(2)}, u32[]{:S(2)}) collective-permute-start(bf16[4,80,2944]{2,1,0:T(8,128)(2,1)} %get-tuple-element.63), channel_id=1, source_target_pairs={{0,1},{1,0},{2,3},{3,2},{4,5},{5,4},{6,7},{7,6},{8,9},{9,8},{10,11... | collective-permute-start | bytes 5652488 | tf_op jit(solution)/shard_map/ppermute | solution.py:364
  312.7 11.1 %collective-permute-start.36 = (bf16[4,80,2944]{2,1,0:T(8,128)(2,1)}, bf16[4,80,2944]{2,1,0:T(8,128)(2,1)S(1)}, u32[]{:S(2)}, u32[]{:S(2)}) collective-permute-start(bf16[4,80,2944]{2,1,0:T(8,128)(2,1)} %get-tuple-element.68), channel_id=1, source_target_pairs={{0,1},{1,0},{2,3},{3,2},{4,5},{5,4},{6,7},{7,6},{8,9},{9,8},{10,11... | collective-permute-start | bytes 5652488 | tf_op jit(solution)/shard_map/ppermute | solution.py:364
  323.7 24.8 %collective-permute-start.33 = (bf16[256,2944]{1,0:T(8,128)(2,1)}, bf16[256,2944]{1,0:T(8,128)(2,1)S(1)}, u32[]{:S(2)}, u32[]{:S(2)}) collective-permute-start(bf16[256,2944]{1,0:T(8,128)(2,1)} %get-tuple-element.65), channel_id=1, source_target_pairs={{0,16},{1,9},{2,18},{3,11},{4,20},{5,13},{6,22},{7,15},{8,24},{9,1... | collective-permute-start | bytes 4521992 | tf_op jit(solution)/shard_map/ppermute | solution.py:420
  331.3 49.5 %collective-permute-start.37 = (bf16[256,2944]{1,0:T(8,128)(2,1)}, bf16[256,2944]{1,0:T(8,128)(2,1)S(1)}, u32[]{:S(2)}, u32[]{:S(2)}) collective-permute-start(bf16[256,2944]{1,0:T(8,128)(2,1)} %get-tuple-element.70), channel_id=1, source_target_pairs={{0,16},{1,9},{2,18},{3,11},{4,20},{5,13},{6,22},{7,15},{8,24},{9,1... | collective-permute-start | bytes 4521992 | tf_op jit(solution)/shard_map/ppermute | solution.py:420
  332.8 61.0 %collective-permute-start.19 = (bf16[128,2944]{1,0:T(8,128)(2,1)S(1)}, bf16[128,2944]{1,0:T(8,128)(2,1)S(1)}, u32[]{:S(2)}, u32[]{:S(2)}) collective-permute-start(bf16[128,2944]{1,0:T(8,128)(2,1)S(1)} %add_convert_fusion.7), channel_id=1, source_target_pairs={{0,8},{1,17},{2,10},{3,19},{4,12},{5,21},{6,14},{7,23},{8,0},{9,25... | collective-permute-start | bytes 2261000 | tf_op jit(solution)/shard_map/ppermute | solution.py:420
  334.5 46.2 %copy-start.7 = (bf16[256,2944]{1,0:T(8,128)(2,1)S(1)}, bf16[256,2944]{1,0:T(8,128)(2,1)}, u32[]{:S(2)}) copy-start(bf16[256,2944]{1,0:T(8,128)(2,1)} %get-tuple-element.69) | copy-start | bytes 4521988
  334.5 47.9 %collective-permute-start.22 = (bf16[128,2944]{1,0:T(8,128)(2,1)S(1)}, bf16[128,2944]{1,0:T(8,128)(2,1)S(1)}, u32[]{:S(2)}, u32[]{:S(2)}) collective-permute-start(bf16[128,2944]{1,0:T(8,128)(2,1)S(1)} %add_convert_fusion.5), channel_id=1, source_target_pairs={{0,8},{1,17},{2,10},{3,19},{4,12},{5,21},{6,14},{7,23},{8,0},{9,25... | collective-permute-start | bytes 2261000 | tf_op jit(solution)/shard_map/ppermute | solution.py:420
  348.6 36.5 %collective-permute-start.34 = (bf16[128,2944]{1,0:T(8,128)(2,1)S(1)}, bf16[128,2944]{1,0:T(8,128)(2,1)S(1)}, u32[]{:S(2)}, u32[]{:S(2)}) collective-permute-start(bf16[128,2944]{1,0:T(8,128)(2,1)S(1)} %add_convert_fusion.3), channel_id=1, source_target_pairs={{0,8},{1,17},{2,10},{3,19},{4,12},{5,21},{6,14},{7,23},{8,0},{9,25... | collective-permute-start | bytes 2261000 | tf_op jit(solution)/shard_map/ppermute | solution.py:420
  380.9 11.1 %collective-permute-start.38 = (bf16[128,2944]{1,0:T(8,128)(2,1)S(1)}, bf16[128,2944]{1,0:T(8,128)(2,1)S(1)}, u32[]{:S(2)}, u32[]{:S(2)}) collective-permute-start(bf16[128,2944]{1,0:T(8,128)(2,1)S(1)} %add_convert_fusion.1), channel_id=1, source_target_pairs={{0,8},{1,17},{2,10},{3,19},{4,12},{5,21},{6,14},{7,23},{8,0},{9,25... | collective-permute-start | bytes 2261000 | tf_op jit(solution)/shard_map/ppermute | solution.py:420
  382.7 50.1 %collective-permute-start.23 = (bf16[128,2944]{1,0:T(8,128)(2,1)S(1)}, bf16[128,2944]{1,0:T(8,128)(2,1)S(1)}, u32[]{:S(2)}, u32[]{:S(2)}) collective-permute-start(bf16[128,2944]{1,0:T(8,128)(2,1)S(1)} %add_convert_fusion.4), channel_id=1, source_target_pairs={{0,4},{2,6},{4,0},{6,2},{1,5},{3,7},{5,1},{7,3},{8,12},{10,14},{12... | collective-permute-start | bytes 2261000 | tf_op jit(solution)/shard_map/ppermute | solution.py:364
  385.4 65.5 %collective-permute-start.35 = (bf16[128,2944]{1,0:T(8,128)(2,1)S(1)}, bf16[128,2944]{1,0:T(8,128)(2,1)S(1)}, u32[]{:S(2)}, u32[]{:S(2)}) collective-permute-start(bf16[128,2944]{1,0:T(8,128)(2,1)S(1)} %add_convert_fusion.2), channel_id=1, source_target_pairs={{0,6},{2,4},{4,2},{6,0},{1,7},{3,5},{5,3},{7,1},{8,14},{10,12},{12... | collective-permute-start | bytes 2261000 | tf_op jit(solution)/shard_map/ppermute | solution.py:364
  392.3 58.7 %collective-permute-start.39 = (bf16[128,2944]{1,0:T(8,128)(2,1)S(1)}, bf16[128,2944]{1,0:T(8,128)(2,1)S(1)}, u32[]{:S(2)}, u32[]{:S(2)}) collective-permute-start(bf16[128,2944]{1,0:T(8,128)(2,1)S(1)} %add_convert_fusion), channel_id=1, source_target_pairs={{0,2},{2,0},{4,6},{6,4},{1,3},{3,1},{5,7},{7,5},{8,10},{10,8},{12,... | collective-permute-start | bytes 2261000 | tf_op jit(solution)/shard_map/ppermute | solution.py:364
  432.8 18.1 %copy-start.8 = (bf16[128,2944]{1,0:T(8,128)(2,1)}, bf16[128,2944]{1,0:T(8,128)(2,1)S(1)}, u32[]{:S(2)}) copy-start(bf16[128,2944]{1,0:T(8,128)(2,1)S(1)} %collective-permute-done.23.refs_1_) | copy-start | bytes 2260996
  (29 other events, 175.3 us)
where the time goes:
time: 462 us; the launch traced here: 456 us
  waiting for transfers between devices  226 us (49%)
  Pallas kernels  149 us (32%)
  starting transfers between devices  47.2 us (10%)
  matrix products  15.9 us (3%)
  local copies, waits for them, and re-layouts  14 us (3%)
    ppermute x20, waiting for transfers between devices, to(): return lax.ppermute(value, everyone, pairs)  138 us
    ppermute x20, waiting for transfers between devices, exchange(): return lax.ppermute(value, axes, [(i, i ^ step) for i in range(count)])  88.2 us
    pallas_call x2, Pallas kernels, run_experts(): pl.pallas_call(functools.partial(expert_kernel, groups=groups), grid=(loc...  49.5 us
    pallas_call x4, Pallas kernels, attend_group(): pl.pallas_call(body, grid_spec=pltpu.PrefetchScalarGridSpec(num_scalar_pr...  43.4 us
    ppermute x20, starting transfers between devices, exchange(): return lax.ppermute(value, axes, [(i, i ^ step) for i in range(count)])  30.6 us
    pallas_call x4, Pallas kernels, spread_rows(): pl.pallas_call(spread_kernel, in_specs=[vmem] * 3 + [pl.BlockSpec(memory_...  24.2 us
    pallas_call x4, Pallas kernels, pick_rows(): pl.pallas_call(functools.partial(pick_kernel, count=count, local=local, w...  23.3 us
    ppermute x20, starting transfers between devices, to(): return lax.ppermute(value, everyone, pairs)  16.5 us
  transfers between devices with their start and end apart: 40, of which 21 were waited for; matrix products, arithmetic and copies ran while one was open for 5% of the time, Pallas kernels for 22%

commit v1 on v0

--- a/solution.py
+++ b/solution.py
@@ -238,15 +238,17 @@
 
 def pick_rows(bases, pieces, local, width, before=(), later=()):
     count = len(pieces)
-    each, wide = pieces[0].shape
+    each, wide = pieces[0][0].shape
     slots = count * CAP
     smem = pl.BlockSpec(memory_space=pltpu.SMEM)
     vmem = pl.BlockSpec(memory_space=pltpu.VMEM)
     hand_on = pl.BlockSpec(memory_space=pl.ANY)
+    spots = [pl.BlockSpec((each, wide), functools.partial(lambda at, i: (at, 0), at)) for _, at in pieces]
     x = jax.ShapeDtypeStruct((local, slots, wide), BF16)
     return pl.pallas_call(
         functools.partial(pick_kernel, count=count, local=local, width=width),
-        in_specs=[smem] + [vmem] * count + [hand_on] * (len(before) + len(later)),
+        grid=(1,),
+        in_specs=[smem] + spots + [hand_on] * (len(before) + len(later)),
         out_specs=[hand_on] * len(later) + [vmem] * 3,
         out_shape=[jax.ShapeDtypeStruct(p.shape, p.dtype) for p in later]
         + [x, x, jax.ShapeDtypeStruct((count * each, 2 * local * slots), BF16)],
@@ -258,12 +260,12 @@
             transcendentals=0,
         ),
         name="pick",
-    )(bases, *pieces, *before, *later)
-
-
-def expert_kernel(bases_s, *refs, groups):
+    )(bases, *[piece for piece, _ in pieces], *before, *later)
+
+
+def expert_kernel(bases_s, *refs, groups, far_parts):
     xs, (up_ref, down_ref) = refs[:groups], refs[groups : groups + 2]
-    ys, acc_ref = refs[-1 - groups : -1], refs[-1]
+    mine_ref, far_refs, acc_ref = refs[-2 - far_parts], refs[-1 - far_parts : -1], refs[-1]
     part_at = pl.program_id(1)
     width = down_ref.shape[1]
     wide = xs[0].shape[2]
@@ -290,35 +292,36 @@
         mine = (lane >= 0) & (lane < TOP) & (info == expert)
         share = jnp.sum(jnp.where(mine, share, 0.0), axis=1, keepdims=True)
         slots = xs[0].shape[1]
-        for i, y_ref in enumerate(ys):
+        per_far = groups // 2 // far_parts
+        for i in range(groups):
             at = slice(i * slots, (i + 1) * slots)
-            y_ref[0, :, :width] = ((acc_ref[at] + part[at]) * share[at]).astype(BF16)
+            y = ((acc_ref[at] + part[at]) * share[at]).astype(BF16)
+            chunk = i // 2
+            y_ref, place = (far_refs[chunk // per_far], chunk % per_far) if i % 2 else (mine_ref, chunk)
+            to = slice(place * slots, (place + 1) * slots)
+            y_ref[0, to, :width] = y
             if wide > width:
-                y_ref[0, :, width:] = jnp.zeros((slots, wide - width), BF16)
-
-
-def run_experts(bases, xs, gate_up, down_t, before=(), later=()):
+                y_ref[0, to, width:] = jnp.zeros((slots, wide - width), BF16)
+
+
+def run_experts(bases, xs, gate_up, down_t, far_parts):
     groups = len(xs)
     local, slots, wide = xs[0].shape
     width, units = gate_up.shape[2:]
     splits = 2
     unit = units // splits
-    x_spec = pl.BlockSpec((1, slots, wide), lambda e, i: (e, 0, 0))
-    hand_on = pl.BlockSpec(memory_space=pl.ANY)
-    return pl.pallas_call(
-        functools.partial(expert_kernel, groups=groups),
+    heights = [groups // 2 * slots] + [groups // 2 // far_parts * slots] * far_parts
+    return pl.pallas_call(
+        functools.partial(expert_kernel, groups=groups, far_parts=far_parts),
         grid=(local, splits),
         in_specs=[
             pl.BlockSpec(memory_space=pltpu.SMEM),
-            *[x_spec] * groups,
+            *[pl.BlockSpec((1, slots, wide), lambda e, i: (e, 0, 0))] * groups,
             pl.BlockSpec((1, 2, width, unit), lambda e, i: (e, 0, 0, i)),
             pl.BlockSpec((1, width, unit), lambda e, i: (e, 0, i)),
-            *[hand_on] * (len(before) + len(later)),
         ],
-        out_specs=[hand_on] * len(later) + [x_spec] * groups,
-        out_shape=[jax.ShapeDtypeStruct(p.shape, p.dtype) for p in later]
-        + [jax.ShapeDtypeStruct((local, slots, wide), BF16)] * groups,
-        input_output_aliases={3 + groups + len(before) + i: i for i in range(len(later))},
+        out_specs=[pl.BlockSpec((1, h, wide), lambda e, i: (e, 0, 0)) for h in heights],
+        out_shape=[jax.ShapeDtypeStruct((local, h, wide), BF16) for h in heights],
         scratch_shapes=[pltpu.VMEM((groups * slots, width), F32)],
         compiler_params=params(VMEM_MIB),
         cost_estimate=pl.CostEstimate(
@@ -327,37 +330,51 @@
             transcendentals=0,
         ),
         name="experts",
-    )(bases, *xs, gate_up, down_t, *before, *later)
-
-
-def spread_kernel(hot_ref, mine_ref, far_ref, *refs):
+    )(bases, *xs, gate_up, down_t)
+
+
+def spread_kernel(*refs, count):
+    hots, (mine_ref, far_ref) = refs[:count], refs[count : count + 2]
     leave_ref, keep_ref = refs[-2:]
+    each = hots[0].shape[0] // len(BACK)
     local, slots, wide = mine_ref.shape
-    y = [ref[...].reshape(local * slots, wide) for ref in (mine_ref, far_ref)]
-    y = jnp.concatenate(y, axis=0)
-    half = leave_ref.shape[0]
-    for i, ref in enumerate((leave_ref, keep_ref)):
-        hot = hot_ref[i * half : (i + 1) * half, :]
-        ref[...] = jnp.dot(hot, y, preferred_element_type=F32).astype(BF16)
-
-
-def spread_rows(hot, mine, far, before=()):
-    rows = hot.shape[0]
-    wide = mine.shape[2]
+    slots = slots // count
+    for c in range(count):
+        y = [
+            ref[:, c * slots : (c + 1) * slots, :].reshape(local * slots, wide)
+            for ref in (mine_ref, far_ref)
+        ]
+        y = jnp.concatenate(y, axis=0)
+        for i in range(2):
+            hot = hots[c][2 * i * each : 2 * (i + 1) * each, :]
+            total = jnp.dot(hot, y, preferred_element_type=F32).astype(BF16)
+            for j in range(2):
+                at = (j * count + c) * each
+                ref = (leave_ref, keep_ref)[i]
+                ref[at : at + each, :] = total[j * each : (j + 1) * each]
+
+
+def spread_rows(hots, mine, far, first, before=()):
+    count = len(hots)
+    rows, depth = hots[0].shape
+    local, height, wide = far.shape
     vmem = pl.BlockSpec(memory_space=pltpu.VMEM)
     return pl.pallas_call(
-        spread_kernel,
-        in_specs=[vmem] * 3 + [pl.BlockSpec(memory_space=pl.ANY)] * len(before),
+        functools.partial(spread_kernel, count=count),
+        grid=(1,),
+        in_specs=[vmem] * count
+        + [pl.BlockSpec((local, height, wide), lambda i: (0, first // count, 0)), vmem]
+        + [pl.BlockSpec(memory_space=pl.ANY)] * len(before),
         out_specs=[vmem] * 2,
-        out_shape=[jax.ShapeDtypeStruct((rows // 2, wide), BF16)] * 2,
+        out_shape=[jax.ShapeDtypeStruct((count * rows // 2, wide), BF16)] * 2,
         compiler_params=params(VMEM_MIB),
         cost_estimate=pl.CostEstimate(
-            flops=4 * hot.size * wide,
-            bytes_accessed=2 * (2 * mine.size + rows * wide),
+            flops=4 * count * rows * depth * wide,
+            bytes_accessed=2 * (2 * far.size + count * rows * wide),
             transcendentals=0,
         ),
         name="spread",
-    )(hot, mine, far, *before)
+    )(*hots, mine, far, *before)
 
 
 def exchange(value, axes, count, step):
@@ -369,6 +386,24 @@
     for term in terms[1:]:
         total = total + term.astype(F32)
     return total.astype(BF16)
+
+
+def turn_kernel(keep_ref, came_ref, *refs):
+    refs[-1][...] = add(keep_ref[...], came_ref[...])
+
+
+def turn_rows(keep, came, before):
+    rows, wide = keep.shape
+    half = pl.BlockSpec((rows // 2, wide), lambda i: (1, 0))
+    return pl.pallas_call(
+        turn_kernel,
+        grid=(1,),
+        in_specs=[half, half] + [pl.BlockSpec(memory_space=pl.ANY)] * len(before),
+        out_specs=pl.BlockSpec((rows // 2, wide), lambda i: (0, 0)),
+        out_shape=jax.ShapeDtypeStruct((rows // 2, wide), BF16),
+        compiler_params=params(VMEM_MIB),
+        name="turn",
+    )(keep, came, *before)
 
 
 def attention_and_norm(
@@ -427,38 +462,41 @@
     each = normed.shape[0]
     down_t = jnp.swapaxes(down_proj, 1, 2)
     rows = {0: normed, 1: to(normed, "z", 1), 2: to(normed, "z", 2)}
-    pairs = ((0, 2), (3, 1))
-    near, sums, cames = {}, [], []
-    for pair in pairs:
-        xs, hots = [], []
-        for r in pair:
-            if r not in near:
-                near[r] = (to(rows[r], "first"), to(rows[r], "second"))
-            plane = [rows[r], *near[r], to(near[r][0], "second")]
-            if r == 0:
-                later = [rows[1], rows[2]]
-                rows[1], rows[2], x, far, hot = pick_rows(bases, plane, local, width, (), later)
-                rows[3] = to(rows[2], "z", 1)
-                near[1] = (to(rows[1], "first"), to(rows[1], "second"))
-            elif r == 2:
-                rows[3], x, far, hot = pick_rows(bases, plane, local, width, (), [rows[3]])
-                near[3] = (to(rows[3], "first"), to(rows[3], "second"))
-            else:
-                x, far, hot = pick_rows(bases, plane, local, width)
-            xs += [x, to(far, "core")]
-            hots.append(hot)
-        if pair == pairs[0]:
-            ys = run_experts(bases, xs, gate_up, down_t)
+
+    def gather(values):
+        one = to(values, "first")
+        return values, one, to(values, "second"), to(one, "second")
+
+    def pick(r, arrays, at, **order):
+        pieces = [(rows[r], 0)] + [(array, at) for array in arrays[1:]]
+        *later, x, far, hot = pick_rows(bases, pieces, local, width, **order)
+        return later, [x, to(far, "core")], hot
+
+    def reduce(hots, mine, far, first, before=(), turn_before=()):
+        count = len(hots)
+        half = count * each
+        leave, keep = spread_rows(hots, mine, to(far, "core"), first, before)
+        came = to(leave, "second")
+        if turn_before:
+            last = to(turn_rows(keep, came, turn_before), "first")
         else:
-            ys = run_experts(bases, xs, gate_up, down_t, before=cames)
-        for at, r in enumerate(pair):
-            y, far = ys[2 * at], to(ys[2 * at + 1], "core")
-            leave, keep = spread_rows(hots[at], y, far)
-            came = to(leave, "second")
-            cames.append(came)
-            last = to(add(keep[each:], came[each:]), "first")
-            total = add(keep[:each], came[:each], last)
-            sums.append(to(total, "z", r) if r else total)
+            last = to(add(keep[half:], came[half:]), "first")
+        parts = [slice(c * each, (c + 1) * each) for c in range(count)]
+        return [add(keep[at], came[at], last[at]) for at in parts], last
+
+    (rows[1], rows[2]), x_0, hot_0 = pick(0, gather(rows[0]), 0, later=[rows[1], rows[2]])
+    rows[3] = to(rows[2], "z", 1)
+    (rows[3],), x_2, hot_2 = pick(2, gather(rows[2]), 0, later=[rows[3]])
+    mine, far = run_experts(bases, x_0 + x_2, gate_up, down_t, 1)
+    (sum_0, sum_2), last = reduce([hot_0, hot_2], mine, far, 0)
+    plane = gather(jnp.concatenate([rows[3], rows[1]], axis=0))
+    _, x_3, hot_3 = pick(3, plane, 0)
+    _, x_1, hot_1 = pick(1, plane, 1)
+    mine, far_3, far_1 = run_experts(bases, x_3 + x_1, gate_up, down_t, 2)
+    sum_2 = to(sum_2, "z", 2)
+    (sum_3,), _ = reduce([hot_3], mine, far_3, 0)
+    (sum_1,), _ = reduce([hot_1], mine, far_1, 1, [last], [sum_2])
+    sums = [sum_0, sum_2, to(sum_3, "z", 3), to(sum_1, "z", 1)]
     return jnp.swapaxes(finish(mixed, sums), 0, 1)
 
 

time: 462 us -> 420 us (0.909)
  the two profiles are of different devices: /device:TPU:13 before, /device:TPU:0 now
where the time goes in v1:
time: 420 us; the launch traced here: 413 us
  waiting for transfers between devices  197 us (47%)
  Pallas kernels  149 us (35%)
  starting transfers between devices  27.2 us (6%)
  matrix products  16 us (4%)
  local copies, waits for them, and re-layouts  14.6 us (3%)
  other arithmetic  8.65 us (2%)
    ppermute x15, waiting for transfers between devices, to(): return lax.ppermute(value, everyone, pairs)  117 us
    ppermute x19, waiting for transfers between devices, exchange(): return lax.ppermute(value, axes, [(i, i ^ step) for i in range(count)])  80.3 us
    pallas_call x2, Pallas kernels, run_experts(): pl.pallas_call(functools.partial(expert_kernel, groups=groups, far_parts=...  49.8 us
    pallas_call x4, Pallas kernels, attend_group(): pl.pallas_call(body, grid_spec=pltpu.PrefetchScalarGridSpec(num_scalar_pr...  43.4 us
    pallas_call x4, Pallas kernels, pick_rows(): pl.pallas_call(functools.partial(pick_kernel, count=count, local=local, w...  23.1 us
    pallas_call x3, Pallas kernels, spread_rows(): pl.pallas_call(functools.partial(spread_kernel, count=count), grid=(1,),...  22.4 us
    dot_general x4, matrix products, project(): term = jnp.dot(part, out_proj, preferred_element_type=F32).astype(BF16)  16 us
    ppermute x19, starting transfers between devices, exchange(): return lax.ppermute(value, axes, [(i, i ^ step) for i in range(count)])  15.7 us
  transfers between devices with their start and end apart: 34, of which 15 were waited for; matrix products, arithmetic and copies ran while one was open for 7% of the time, Pallas kernels for 30%

profile of v1, /device:TPU:0, one launch (start us, length us, event | category | flops | bytes accessed | tf_op | source)
XLA Modules:
  0.0 413.0 jit_solution(12300067291234679223)
XLA Ops:
  1.3 10.8 %attend.4 = bf16[128,1024]{1,0:T(8,128)(2,1)} custom-call(s32[1]{0:T(128)} %bitcast.1.col_s, s32[4]{0:T(128)} %rows_s.7, s32[4]{0:T(128)} %ctx_s.7, s32[16]{0:T(128)} %reshape.22.table_s, f32[64]{0:T(128)} %sink_s.7, bf16[128,4096]{1,0:T(8,128)(2,1)} %q_ref.7, bf16[16,128,1024]{2,1,0:T(8,128)(2,1)} %kv_ref.7), custom_call_target="tpu_custom_call" | custom-call | flops 2147483648 | bytes 1572864 | tf_op jit(solution)/shard_map/attend/pallas_call | solution.py:110
  12.1 3.9 collective-permute-start
  16.0 11.0 %attend.5 = bf16[128,1024]{1,0:T(8,128)(2,1)} custom-call(s32[1]{0:T(128)} %bitcast.3.col_s, s32[4]{0:T(128)} %rows_s.7, s32[4]{0:T(128)} %ctx_s.7, s32[16]{0:T(128)} %reshape.22.table_s, f32[64]{0:T(128)} %sink_s.7, bf16[128,4096]{1,0:T(8,128)(2,1)} %q_ref.7, bf16[16,128,1024]{2,1,0:T(8,128)(2,1)} %kv_ref.7), custom_call_target="tpu_custom_call" | custom-call | flops 2147483648 | bytes 1572864 | tf_op jit(solution)/shard_map/attend/pallas_call | solution.py:110
  27.0 5.5 %fusion.refs_0_ = bf16[2880,128]{1,0:T(8,128)(2,1)} fusion(bf16[128,1024]{1,0:T(8,128)(2,1)} %collective-permute-done, bf16[1024,2880]{0,1:T(8,128)(2,1)} %param.20), kind=kOutput, calls=%fused_computation.4 | convolution fusion | flops 755343360 | bytes 6897664 | tf_op jit(solution)/shard_map/dot_general | solution.py:423
  33.2 10.8 %attend.6 = bf16[128,1024]{1,0:T(8,128)(2,1)} custom-call(s32[1]{0:T(128)} %bitcast.5.col_s, s32[4]{0:T(128)} %rows_s.7, s32[4]{0:T(128)} %ctx_s.7, s32[16]{0:T(128)} %reshape.22.table_s, f32[64]{0:T(128)} %sink_s.7, bf16[128,4096]{1,0:T(8,128)(2,1)} %q_ref.7, bf16[16,128,1024]{2,1,0:T(8,128)(2,1)} %kv_ref.7, bf16[2880,128]{1,0:T(8,128)(2,1)} %fusion.refs_0_), custom_call_target="tpu_custom_call" | custom-call | flops 2147483648 | bytes 1572864 | tf_op jit(solution)/shard_map/attend/pallas_call | solution.py:110
  44.0 1.5 collective-permute-start.4
  45.6 2.6 fusion.1.refs_0_
  49.3 8.0 %collective-permute-done.4 = bf16[128,1024]{1,0:T(8,128)(2,1)S(1)} collective-permute-done((bf16[128,1024]{1,0:T(8,128)(2,1)}, bf16[128,1024]{1,0:T(8,128)(2,1)S(1)}, u32[]{:S(2)}, u32[]{:S(2)}) %collective-permute-start.4) | collective-permute-done | bytes 262176 | tf_op jit(solution)/shard_map/ppermute | solution.py:381
  57.4 2.6 fusion.2
  61.9 10.8 %attend.7 = bf16[128,1024]{1,0:T(8,128)(2,1)} custom-call(s32[1]{0:T(128)} %bitcast.7.col_s, s32[4]{0:T(128)} %rows_s.7, s32[4]{0:T(128)} %ctx_s.7, s32[16]{0:T(128)} %reshape.22.table_s, f32[64]{0:T(128)} %sink_s.7, bf16[128,4096]{1,0:T(8,128)(2,1)} %q_ref.7, bf16[16,128,1024]{2,1,0:T(8,128)(2,1)} %kv_ref.7, bf16[2880,128]{1,0:T(8,128)(2,1)} %fusion.1.refs_0_), custom_call_target="tpu_custom_call" | custom-call | flops 2147483648 | bytes 1572864 | tf_op jit(solution)/shard_map/attend/pallas_call | solution.py:110
  72.7 5.3 %fusion.3.d_ref = bf16[2880,128]{1,0:T(8,128)(2,1)} fusion(bf16[128,1024]{1,0:T(8,128)(2,1)} %attend.7, bf16[1024,2880]{0,1:T(8,128)(2,1)} %param.20), kind=kOutput, calls=%fused_computation.7 | convolution fusion | flops 755343360 | bytes 6897664 | tf_op jit(solution)/shard_map/dot_general | solution.py:423
  78.9 4.7 %mix_norm.1 = (bf16[2880,128]{1,0:T(8,128)(2,1)}, bf16[128,2944]{1,0:T(8,128)(2,1)}) custom-call(bf16[2880,128]{1,0:T(8,128)(2,1)} %bitcast.27, bf16[2880,128]{1,0:T(8,128)(2,1)} %collective-permute-done.1.a_ref, bf16[2880,128]{1,0:T(8,128)(2,1)} %collective-permute-done.3.b_ref, bf16[2880,128]{1,0:T(8,128)(2,1)} %copy-done.12, ...), custom_call_target="tpu_custom_call" | custom-call | tf_op jit(solution)/shard_map/mix_norm/pallas_call | solution.py:163
  85.7 1.6 collective-permute-start.9
  87.2 2.6 collective-permute-start.10
  89.8 12.3 %collective-permute-done.6.refs_1_ = bf16[128,2944]{1,0:T(8,128)(2,1)S(1)} collective-permute-done((bf16[128,2944]{1,0:T(8,128)(2,1)}, bf16[128,2944]{1,0:T(8,128)(2,1)S(1)}, u32[]{:S(2)}, u32[]{:S(2)}) %collective-permute-start.6) | collective-permute-done | bytes 753696 | tf_op jit(solution)/shard_map/ppermute | solution.py:455
  102.1 1.8 collective-permute-start.8
  104.5 14.2 %collective-permute-done.9.refs_4_ = bf16[128,2944]{1,0:T(8,128)(2,1)S(1)} collective-permute-done((bf16[128,2944]{1,0:T(8,128)(2,1)}, bf16[128,2944]{1,0:T(8,128)(2,1)S(1)}, u32[]{:S(2)}, u32[]{:S(2)}) %collective-permute-start.9) | collective-permute-done | bytes 753696 | tf_op jit(solution)/shard_map/ppermute | solution.py:381
  118.8 1.9 collective-permute-done.10.refs_5_
  121.5 5.8 %pick.4 = (bf16[128,2944]{1,0:T(8,128)(2,1)}, bf16[128,2944]{1,0:T(8,128)(2,1)}, bf16[4,80,2944]{2,1,0:T(8,128)(2,1)}, bf16[4,80,2944]{2,1,0:T(8,128)(2,1)}, bf16[512,640]{1,0:T(8,128)(2,1)}) custom-call(s32[2]{0:T(128)} %fusion.4.bases_s, bf16[128,2944]{1,0:T(8,128)(2,1)} %get-tuple-element.34.refs_0_, ...), custom_call_target="tpu_custom_call", output_to_operand_aliasing={{0}: (5, {}), {1}: (6, {})} | custom-call | flops 3858759680 | bytes 6782976 | tf_op jit(solution)/shard_map/pick/pallas_call | solution.py:248
  127.8 1.5 collective-permute-start.12
  129.7 17.5 %collective-permute-done.11.refs_1_ = bf16[128,2944]{1,0:T(8,128)(2,1)S(1)} collective-permute-done((bf16[128,2944]{1,0:T(8,128)(2,1)}, bf16[128,2944]{1,0:T(8,128)(2,1)S(1)}, u32[]{:S(2)}, u32[]{:S(2)}) %collective-permute-start.11) | collective-permute-done | bytes 753696 | tf_op jit(solution)/shard_map/ppermute | solution.py:455
  147.3 11.6 %collective-permute-done.13.refs_3_ = bf16[128,2944]{1,0:T(8,128)(2,1)S(1)} collective-permute-done((bf16[128,2944]{1,0:T(8,128)(2,1)S(1)}, bf16[128,2944]{1,0:T(8,128)(2,1)S(1)}, u32[]{:S(2)}, u32[]{:S(2)}) %collective-permute-start.13) | collective-permute-done | bytes 753696 | tf_op jit(solution)/shard_map/ppermute | solution.py:455
  159.8 5.8 %pick.5 = (bf16[128,2944]{1,0:T(8,128)(2,1)}, bf16[4,80,2944]{2,1,0:T(8,128)(2,1)}, bf16[4,80,2944]{2,1,0:T(8,128)(2,1)}, bf16[512,640]{1,0:T(8,128)(2,1)}) custom-call(s32[2]{0:T(128)} %fusion.4.bases_s, bf16[128,2944]{1,0:T(8,128)(2,1)} %get-tuple-element.36.refs_0_, bf16[128,2944]{1,0:T(8,128)(2,1)} %copy-done.23, ...), custom_call_target="tpu_custom_call", output_to_operand_aliasing={{0}: (5, {})} | custom-call | flops 3858759680 | bytes 6782976 | tf_op jit(solution)/shard_map/pick/pallas_call | solution.py:248
  167.6 2.0 collective-permute-done.16.refs_3_
  170.9 24.8 %experts.2 = (bf16[4,160,2944]{2,1,0:T(8,128)(2,1)}, bf16[4,160,2944]{2,1,0:T(8,128)(2,1)}) custom-call(s32[2]{0:T(128)} %fusion.4.bases_s, bf16[4,80,2944]{2,1,0:T(8,128)(2,1)} %get-tuple-element.38.refs_0_, bf16[4,80,2944]{2,1,0:T(8,128)(2,1)} %copy-done.17, bf16[4,80,2944]{2,1,0:T(8,128)(2,1)} %get-tuple-element.40.refs_2_, ...), custom_call_target="tpu_custom_call" | custom-call | flops 22649241600 | bytes 50462720 | tf_op jit(solution)/shard_map/experts/pallas_call | solution.py:314
  195.9 2.0 collective-permute-start.23
  197.9 17.7 %collective-permute-done.22.refs_2_ = bf16[256,2944]{1,0:T(8,128)(2,1)S(1)} collective-permute-done((bf16[256,2944]{1,0:T(8,128)(2,1)S(1)}, bf16[256,2944]{1,0:T(8,128)(2,1)S(1)}, u32[]{:S(2)}, u32[]{:S(2)}) %collective-permute-start.22) | collective-permute-done | bytes 1507360 | tf_op jit(solution)/shard_map/ppermute | solution.py:455
  216.8 15.1 %collective-permute-done.23.refs_3_ = bf16[256,2944]{1,0:T(8,128)(2,1)} collective-permute-done((bf16[256,2944]{1,0:T(8,128)(2,1)}, bf16[256,2944]{1,0:T(8,128)(2,1)}, u32[]{:S(2)}, u32[]{:S(2)}) %collective-permute-start.23) | collective-permute-done | bytes 1507360 | tf_op jit(solution)/shard_map/ppermute | solution.py:455
  231.8 5.7 %pick.6 = (bf16[4,80,2944]{2,1,0:T(8,128)(2,1)}, bf16[4,80,2944]{2,1,0:T(8,128)(2,1)}, bf16[512,640]{1,0:T(8,128)(2,1)}) custom-call(s32[2]{0:T(128)} %fusion.4.bases_s, bf16[128,2944]{1,0:T(8,128)(2,1)} %get-tuple-element.46.refs_0_, bf16[256,2944]{1,0:T(8,128)(2,1)} %collective-permute-done.21.refs_1_, bf16[256,2944]{1,0:T(8,128)(2,1)} %copy-done.19, ...), custom_call_target="tpu_custom_call" | custom-call | flops 3858759680 | bytes 6782976 | tf_op jit(solution)/shard_map/pick/pallas_call | solution.py:248
  237.6 5.8 %pick.7 = (bf16[4,80,2944]{2,1,0:T(8,128)(2,1)}, bf16[4,80,2944]{2,1,0:T(8,128)(2,1)}, bf16[512,640]{1,0:T(8,128)(2,1)}) custom-call(s32[2]{0:T(128)} %fusion.4.bases_s, bf16[128,2944]{1,0:T(8,128)(2,1)} %get-tuple-element.47.refs_0_, bf16[256,2944]{1,0:T(8,128)(2,1)} %collective-permute-done.21.refs_1_, bf16[256,2944]{1,0:T(8,128)(2,1)} %copy-done.19, ...), custom_call_target="tpu_custom_call" | custom-call | flops 3858759680 | bytes 6782976 | tf_op jit(solution)/shard_map/pick/pallas_call | solution.py:248
  243.9 1.9 copy-done.16
  245.8 10.3 %spread.3 = (bf16[512,2944]{1,0:T(8,128)(2,1)}, bf16[512,2944]{1,0:T(8,128)(2,1)}) custom-call(bf16[512,640]{1,0:T(8,128)(2,1)} %get-tuple-element.35.refs_0_, bf16[512,640]{1,0:T(8,128)(2,1)} %get-tuple-element.37.refs_1_, bf16[4,160,2944]{2,1,0:T(8,128)(2,1)} %get-tuple-element.42.refs_2_, bf16[4,160,2944]{2,1,0:T(8,128)(2,1)} %copy-done.16), custom_call_target="tpu_custom_call" | custom-call | flops 7717519360 | bytes 13565952 | tf_op jit(solution)/shard_map/spread/pallas_call | solution.py:362
  256.1 25.0 %experts.3 = (bf16[4,160,2944]{2,1,0:T(8,128)(2,1)}, bf16[4,80,2944]{2,1,0:T(8,128)(2,1)}, bf16[4,80,2944]{2,1,0:T(8,128)(2,1)}) custom-call(s32[2]{0:T(128)} %fusion.4.bases_s, bf16[4,80,2944]{2,1,0:T(8,128)(2,1)} %get-tuple-element.49.refs_0_, bf16[4,80,2944]{2,1,0:T(8,128)(2,1)} %collective-permute-done.24.refs_1_, ...), custom_call_target="tpu_custom_call" | custom-call | flops 22649241600 | bytes 50462720 | tf_op jit(solution)/shard_map/experts/pallas_call | solution.py:314
  281.7 10.6 %collective-permute-done.18 = bf16[512,2944]{1,0:T(8,128)(2,1)} collective-permute-done((bf16[512,2944]{1,0:T(8,128)(2,1)}, bf16[512,2944]{1,0:T(8,128)(2,1)}, u32[]{:S(2)}, u32[]{:S(2)}) %collective-permute-start.18) | collective-permute-done | bytes 3014688 | tf_op jit(solution)/shard_map/ppermute | solution.py:455
  292.3 1.7 add_convert_fusion
  294.6 6.1 %spread.4 = (bf16[256,2944]{1,0:T(8,128)(2,1)}, bf16[256,2944]{1,0:T(8,128)(2,1)}) custom-call(bf16[512,640]{1,0:T(8,128)(2,1)} %get-tuple-element.48.refs_0_, bf16[4,160,2944]{2,1,0:T(8,128)(2,1)} %get-tuple-element.53.refs_1_, bf16[4,80,2944]{2,1,0:T(8,128)(2,1)} %collective-permute-done.26.refs_2_), custom_call_target="tpu_custom_call" | custom-call | flops 3858759680 | bytes 6782976 | tf_op jit(solution)/shard_map/spread/pallas_call | solution.py:362
  301.0 24.4 %collective-permute-done.19.refs_3_ = bf16[256,2944]{1,0:T(8,128)(2,1)S(1)} collective-permute-done((bf16[256,2944]{1,0:T(8,128)(2,1)S(1)}, bf16[256,2944]{1,0:T(8,128)(2,1)S(1)}, u32[]{:S(2)}, u32[]{:S(2)}) %collective-permute-start.19) | collective-permute-done | bytes 1507360 | tf_op jit(solution)/shard_map/ppermute | solution.py:455
  326.6 6.0 %spread.5 = (bf16[256,2944]{1,0:T(8,128)(2,1)}, bf16[256,2944]{1,0:T(8,128)(2,1)}) custom-call(bf16[512,640]{1,0:T(8,128)(2,1)} %get-tuple-element.57.refs_0_, bf16[4,160,2944]{2,1,0:T(8,128)(2,1)} %get-tuple-element.53.refs_1_, bf16[4,80,2944]{2,1,0:T(8,128)(2,1)} %collective-permute-done.30.refs_2_, bf16[256,2944]{1,0:T(8,128)(2,1)} %copy-done.6), custom_call_target="tpu_custom_call" | custom-call | flops 3858759680 | bytes 6782976 | tf_op jit(solution)/shard_map/spread/pallas_call | solution.py:362
  332.6 3.3 add_convert_fusion.4
  338.2 27.7 %collective-permute-done.20.refs_0_.refs_1_ = bf16[128,2944]{1,0:T(8,128)(2,1)S(1)} collective-permute-done((bf16[128,2944]{1,0:T(8,128)(2,1)S(1)}, bf16[128,2944]{1,0:T(8,128)(2,1)S(1)}, u32[]{:S(2)}, u32[]{:S(2)}) %collective-permute-start.20) | collective-permute-done | bytes 753696 | tf_op jit(solution)/shard_map/ppermute | solution.py:381
  367.3 2.4 turn.1
  369.7 1.6 collective-permute-start.32
  371.3 1.4 add_convert_fusion.2
  372.7 1.5 collective-permute-start.29
  374.2 7.4 %collective-permute-done.32 = bf16[128,2944]{1,0:T(8,128)(2,1)S(1)} collective-permute-done((bf16[128,2944]{1,0:T(8,128)(2,1)}, bf16[128,2944]{1,0:T(8,128)(2,1)S(1)}, u32[]{:S(2)}, u32[]{:S(2)}) %collective-permute-start.32) | collective-permute-done | bytes 753696 | tf_op jit(solution)/shard_map/ppermute | solution.py:455
  381.9 12.5 %collective-permute-done.29.refs_2_ = bf16[128,2944]{1,0:T(8,128)(2,1)S(1)} collective-permute-done((bf16[128,2944]{1,0:T(8,128)(2,1)S(1)}, bf16[128,2944]{1,0:T(8,128)(2,1)S(1)}, u32[]{:S(2)}, u32[]{:S(2)}) %collective-permute-start.29) | collective-permute-done | bytes 753696 | tf_op jit(solution)/shard_map/ppermute | solution.py:381
  394.4 13.9 %collective-permute-done.33.refs_3_ = bf16[128,2944]{1,0:T(8,128)(2,1)S(1)} collective-permute-done((bf16[128,2944]{1,0:T(8,128)(2,1)S(1)}, bf16[128,2944]{1,0:T(8,128)(2,1)S(1)}, u32[]{:S(2)}, u32[]{:S(2)}) %collective-permute-start.33) | collective-permute-done | bytes 753696 | tf_op jit(solution)/shard_map/ppermute | solution.py:381
  409.2 3.4 finish.1
  (111 shorter events, 24.2 us)
Async XLA Ops:
  12.1 14.9 %collective-permute-start = (bf16[128,1024]{1,0:T(8,128)(2,1)}, bf16[128,1024]{1,0:T(8,128)(2,1)}, u32[]{:S(2)}, u32[]{:S(2)}) collective-permute-start(bf16[128,1024]{1,0:T(8,128)(2,1)} %attend.4), channel_id=1, source_target_pairs={{0,24},{8,16},{16,8},{24,0},{1,25},{9,17},{17,9},{25,1},{2,26},{10... | collective-permute-start | bytes 786440 | tf_op jit(solution)/shard_map/ppermute | solution.py:381
  16.0 29.6 %slice-start = ((s8[5898240]{0:T(1024)(128)(4,1)}), s8[1703936]{0:T(1024)(128)(4,1)S(1)}, s32[]{:S(2)}) async-start(s8[5898240]{0:T(1024)(128)(4,1)} %bitcast.25), calls=%async_computation | async-start | bytes 3407872
  26.9 18.6 %collective-permute-start.2 = (bf16[128,1024]{1,0:T(8,128)(2,1)}, bf16[128,1024]{1,0:T(8,128)(2,1)S(1)}, u32[]{:S(2)}, u32[]{:S(2)}) collective-permute-start(bf16[128,1024]{1,0:T(8,128)(2,1)} %attend.5), channel_id=1, source_target_pairs={{0,16},{8,24},{16,0},{24,8},{1,17},{9,25},{17,1},{25,9},{2,18},{10... | collective-permute-start | bytes 786440 | tf_op jit(solution)/shard_map/ppermute | solution.py:381
  26.9 18.6 %slice-start.1 = ((s8[5898240]{0:T(1024)(128)(4,1)}), s8[4194304]{0:T(1024)(128)(4,1)S(1)}, s32[]{:S(2)}) async-start(s8[5898240]{0:T(1024)(128)(4,1)} %bitcast.25), calls=%async_computation.1 | async-start | bytes 8388608
  32.4 45.6 %collective-permute-start.1 = (bf16[2880,128]{1,0:T(8,128)(2,1)}, bf16[2880,128]{1,0:T(8,128)(2,1)}, u32[]{:S(2)}, u32[]{:S(2)}) collective-permute-start(bf16[2880,128]{1,0:T(8,128)(2,1)} %fusion.refs_0_), channel_id=1, source_target_pairs={{0,24},{8,16},{16,8},{24,0},{1,25},{9,17},{17,9},{25,1},{2,26},{10... | collective-permute-start | bytes 2211848 | tf_op jit(solution)/shard_map/ppermute | solution.py:381
  44.0 13.3 %collective-permute-start.4 = (bf16[128,1024]{1,0:T(8,128)(2,1)}, bf16[128,1024]{1,0:T(8,128)(2,1)S(1)}, u32[]{:S(2)}, u32[]{:S(2)}) collective-permute-start(bf16[128,1024]{1,0:T(8,128)(2,1)} %attend.6), channel_id=1, source_target_pairs={{0,8},{8,0},{16,24},{24,16},{1,9},{9,1},{17,25},{25,17},{2,10},{10... | collective-permute-start | bytes 786440 | tf_op jit(solution)/shard_map/ppermute | solution.py:381
  48.1 12.4 %copy-start.13 = (f32[2880]{0:T(1024)S(1)}, f32[2880]{0:T(1024)}, u32[]{:S(2)}) copy-start(f32[2880]{0:T(1024)} %param.21) | copy-start | bytes 34564
  48.1 13.0 %copy-start.14 = (s32[128,4]{0,1:T(4,128)S(1)}, s32[128,4]{0,1:T(4,128)}, u32[]{:S(2)}) copy-start(s32[128,4]{0,1:T(4,128)} %param.22) | copy-start | bytes 6148
  48.1 13.0 %copy-start.15 = (f32[128,4]{0,1:T(4,128)S(1)}, f32[128,4]{0,1:T(4,128)}, u32[]{:S(2)}) copy-start(f32[128,4]{0,1:T(4,128)} %param.23) | copy-start | bytes 6148
  48.1 29.9 %collective-permute-start.3 = (bf16[2880,128]{1,0:T(8,128)(2,1)}, bf16[2880,128]{1,0:T(8,128)(2,1)}, u32[]{:S(2)}, u32[]{:S(2)}) collective-permute-start(bf16[2880,128]{1,0:T(8,128)(2,1)} %fusion.1.refs_0_), channel_id=1, source_target_pairs={{0,16},{8,24},{16,0},{24,8},{1,17},{9,25},{17,1},{25,9},{2,18},{10... | collective-permute-start | bytes 2211848 | tf_op jit(solution)/shard_map/ppermute | solution.py:381
  60.0 18.1 %collective-permute-start.5 = (bf16[2880,128]{1,0:T(8,128)(2,1)}, bf16[2880,128]{1,0:T(8,128)(2,1)S(1)}, u32[]{:S(2)}, u32[]{:S(2)}) collective-permute-start(bf16[2880,128]{1,0:T(8,128)(2,1)} %fusion.2), channel_id=1, source_target_pairs={{0,8},{8,0},{16,24},{24,16},{1,9},{9,1},{17,25},{25,17},{2,10},{10... | collective-permute-start | bytes 2211848 | tf_op jit(solution)/shard_map/ppermute | solution.py:381
  83.7 18.4 %collective-permute-start.6 = (bf16[128,2944]{1,0:T(8,128)(2,1)}, bf16[128,2944]{1,0:T(8,128)(2,1)S(1)}, u32[]{:S(2)}, u32[]{:S(2)}) collective-permute-start(bf16[128,2944]{1,0:T(8,128)(2,1)} %get-tuple-element.34.refs_0_), channel_id=1, source_target_pairs={{0,8},{1,17},{2,10},{3,19},{4,12},{5,21},{6,14},{7,23},{8,0},{9,25... | collective-permute-start | bytes 2261000 | tf_op jit(solution)/shard_map/ppermute | solution.py:455
  84.4 20.1 %collective-permute-start.7 = (bf16[128,2944]{1,0:T(8,128)(2,1)}, bf16[128,2944]{1,0:T(8,128)(2,1)S(1)}, u32[]{:S(2)}, u32[]{:S(2)}) collective-permute-start(bf16[128,2944]{1,0:T(8,128)(2,1)} %get-tuple-element.34.refs_0_), channel_id=1, source_target_pairs={{0,16},{1,9},{2,18},{3,11},{4,20},{5,13},{6,22},{7,15},{8,24},{9,1... | collective-permute-start | bytes 2261000 | tf_op jit(solution)/shard_map/ppermute | solution.py:455
  85.7 33.1 %collective-permute-start.9 = (bf16[128,2944]{1,0:T(8,128)(2,1)}, bf16[128,2944]{1,0:T(8,128)(2,1)S(1)}, u32[]{:S(2)}, u32[]{:S(2)}) collective-permute-start(bf16[128,2944]{1,0:T(8,128)(2,1)} %get-tuple-element.34.refs_0_), channel_id=1, source_target_pairs={{0,2},{2,0},{4,6},{6,4},{1,3},{3,1},{5,7},{7,5},{8,10},{10,8},{12,... | collective-permute-start | bytes 2261000 | tf_op jit(solution)/shard_map/ppermute | solution.py:381
  87.2 33.4 %collective-permute-start.10 = (bf16[128,2944]{1,0:T(8,128)(2,1)}, bf16[128,2944]{1,0:T(8,128)(2,1)S(1)}, u32[]{:S(2)}, u32[]{:S(2)}) collective-permute-start(bf16[128,2944]{1,0:T(8,128)(2,1)} %get-tuple-element.34.refs_0_), channel_id=1, source_target_pairs={{0,4},{2,6},{4,0},{6,2},{1,5},{3,7},{5,1},{7,3},{8,12},{10,14},{12... | collective-permute-start | bytes 2261000 | tf_op jit(solution)/shard_map/ppermute | solution.py:381
  102.1 18.6 %copy-start.20 = (bf16[128,2944]{1,0:T(8,128)(2,1)}, bf16[128,2944]{1,0:T(8,128)(2,1)S(1)}, u32[]{:S(2)}) copy-start(bf16[128,2944]{1,0:T(8,128)(2,1)S(1)} %collective-permute-done.6.refs_1_) | copy-start | bytes 2260996
  102.1 18.6 %collective-permute-start.8 = (bf16[128,2944]{1,0:T(8,128)(2,1)S(1)}, bf16[128,2944]{1,0:T(8,128)(2,1)}, u32[]{:S(2)}, u32[]{:S(2)}) collective-permute-start(bf16[128,2944]{1,0:T(8,128)(2,1)S(1)} %collective-permute-done.6.refs_1_), channel_id=1, source_target_pairs={{0,16},{1,9},{2,18},{3,11},{4,20},{5,13},{6,22},{7,15},{8,24},{9,1... | collective-permute-start | bytes 2261000 | tf_op jit(solution)/shard_map/ppermute | solution.py:455
  104.5 16.1 %copy-start.21 = (bf16[128,2944]{1,0:T(8,128)(2,1)}, bf16[128,2944]{1,0:T(8,128)(2,1)S(1)}, u32[]{:S(2)}) copy-start(bf16[128,2944]{1,0:T(8,128)(2,1)S(1)} %collective-permute-done.7.refs_2_) | copy-start | bytes 2260996
  127.3 20.0 %collective-permute-start.11 = (bf16[128,2944]{1,0:T(8,128)(2,1)}, bf16[128,2944]{1,0:T(8,128)(2,1)S(1)}, u32[]{:S(2)}, u32[]{:S(2)}) collective-permute-start(bf16[128,2944]{1,0:T(8,128)(2,1)} %get-tuple-element.36.refs_0_), channel_id=1, source_target_pairs={{0,8},{1,17},{2,10},{3,19},{4,12},{5,21},{6,14},{7,23},{8,0},{9,25... | collective-permute-start | bytes 2261000 | tf_op jit(solution)/shard_map/ppermute | solution.py:455
  127.8 19.5 %collective-permute-start.12 = (bf16[128,2944]{1,0:T(8,128)(2,1)}, bf16[128,2944]{1,0:T(8,128)(2,1)S(1)}, u32[]{:S(2)}, u32[]{:S(2)}) collective-permute-start(bf16[128,2944]{1,0:T(8,128)(2,1)} %get-tuple-element.36.refs_0_), channel_id=1, source_target_pairs={{0,16},{1,9},{2,18},{3,11},{4,20},{5,13},{6,22},{7,15},{8,24},{9,1... | collective-permute-start | bytes 2261000 | tf_op jit(solution)/shard_map/ppermute | solution.py:455
  129.3 18.0 %collective-permute-start.14 = (bf16[128,2944]{1,0:T(8,128)(2,1)}, bf16[128,2944]{1,0:T(8,128)(2,1)S(1)}, u32[]{:S(2)}, u32[]{:S(2)}) collective-permute-start(bf16[128,2944]{1,0:T(8,128)(2,1)} %get-tuple-element.36.refs_0_), channel_id=1, source_target_pairs={{0,2},{2,0},{4,6},{6,4},{1,3},{3,1},{5,7},{7,5},{8,10},{10,8},{12,... | collective-permute-start | bytes 2261000 | tf_op jit(solution)/shard_map/ppermute | solution.py:381
  147.3 11.6 %copy-start.23 = (bf16[128,2944]{1,0:T(8,128)(2,1)}, bf16[128,2944]{1,0:T(8,128)(2,1)S(1)}, u32[]{:S(2)}) copy-start(bf16[128,2944]{1,0:T(8,128)(2,1)S(1)} %collective-permute-done.11.refs_1_) | copy-start | bytes 2260996
  147.3 11.6 %collective-permute-start.13 = (bf16[128,2944]{1,0:T(8,128)(2,1)S(1)}, bf16[128,2944]{1,0:T(8,128)(2,1)S(1)}, u32[]{:S(2)}, u32[]{:S(2)}) collective-permute-start(bf16[128,2944]{1,0:T(8,128)(2,1)S(1)} %collective-permute-done.11.refs_1_), channel_id=1, source_target_pairs={{0,16},{1,9},{2,18},{3,11},{4,20},{5,13},{6,22},{7,15},{8,24},{9,1... | collective-permute-start | bytes 2261000 | tf_op jit(solution)/shard_map/ppermute | solution.py:455
  147.3 20.3 %collective-permute-start.15 = (bf16[4,80,2944]{2,1,0:T(8,128)(2,1)}, bf16[4,80,2944]{2,1,0:T(8,128)(2,1)S(1)}, u32[]{:S(2)}, u32[]{:S(2)}) collective-permute-start(bf16[4,80,2944]{2,1,0:T(8,128)(2,1)} %get-tuple-element.39), channel_id=1, source_target_pairs={{0,1},{1,0},{2,3},{3,2},{4,5},{5,4},{6,7},{7,6},{8,9},{9,8},{10,11... | collective-permute-start | bytes 5652488 | tf_op jit(solution)/shard_map/ppermute | solution.py:381
  147.3 11.6 %copy-start.24 = (bf16[128,2944]{1,0:T(8,128)(2,1)}, bf16[128,2944]{1,0:T(8,128)(2,1)S(1)}, u32[]{:S(2)}) copy-start(bf16[128,2944]{1,0:T(8,128)(2,1)S(1)} %collective-permute-done.12.refs_2_) | copy-start | bytes 2260996
  147.3 11.6 %copy-start.9 = (bf16[128,2944]{1,0:T(8,128)(2,1)}, bf16[128,2944]{1,0:T(8,128)(2,1)S(1)}, u32[]{:S(2)}) copy-start(bf16[128,2944]{1,0:T(8,128)(2,1)S(1)} %collective-permute-done.14.refs_4_) | copy-start | bytes 2260996
  165.6 4.1 collective-permute-start.16
  167.0 28.9 %collective-permute-start.21 = (bf16[256,2944]{1,0:T(8,128)(2,1)S(1)}, bf16[256,2944]{1,0:T(8,128)(2,1)}, u32[]{:S(2)}, u32[]{:S(2)}) collective-permute-start(bf16[256,2944]{1,0:T(8,128)(2,1)S(1)} %constant_dynamic-update-slice_fusion), channel_id=1, source_target_pairs={{0,8},{1,17},{2,10},{3,19},{4,12},{5,21},{6,14},{7,23},{8,0},{9,25... | collective-permute-start | bytes 4521992 | tf_op jit(solution)/shard_map/ppermute | solution.py:455
  195.7 48.2 %collective-permute-start.17 = (bf16[4,160,2944]{2,1,0:T(8,128)(2,1)}, bf16[4,160,2944]{2,1,0:T(8,128)(2,1)S(1)}, u32[]{:S(2)}, u32[]{:S(2)}) collective-permute-start(bf16[4,160,2944]{2,1,0:T(8,128)(2,1)} %get-tuple-element.43), channel_id=1, source_target_pairs={{0,1},{1,0},{2,3},{3,2},{4,5},{5,4},{6,7},{7,6},{8,9},{9,8},{10,11... | collective-permute-start | bytes 11304968 | tf_op jit(solution)/shard_map/ppermute | solution.py:381
  195.9 19.7 %collective-permute-start.22 = (bf16[256,2944]{1,0:T(8,128)(2,1)S(1)}, bf16[256,2944]{1,0:T(8,128)(2,1)S(1)}, u32[]{:S(2)}, u32[]{:S(2)}) collective-permute-start(bf16[256,2944]{1,0:T(8,128)(2,1)S(1)} %constant_dynamic-update-slice_fusion), channel_id=1, source_target_pairs={{0,16},{1,9},{2,18},{3,11},{4,20},{5,13},{6,22},{7,15},{8,24},{9,1... | collective-permute-start | bytes 4521992 | tf_op jit(solution)/shard_map/ppermute | solution.py:455
  195.9 36.0 %collective-permute-start.23 = (bf16[256,2944]{1,0:T(8,128)(2,1)}, bf16[256,2944]{1,0:T(8,128)(2,1)}, u32[]{:S(2)}, u32[]{:S(2)}) collective-permute-start(bf16[256,2944]{1,0:T(8,128)(2,1)} %collective-permute-done.21.refs_1_), channel_id=1, source_target_pairs={{0,16},{1,9},{2,18},{3,11},{4,20},{5,13},{6,22},{7,15},{8,24},{9,1... | collective-permute-start | bytes 4521992 | tf_op jit(solution)/shard_map/ppermute | solution.py:455
  237.6 18.5 %collective-permute-start.24 = (bf16[4,80,2944]{2,1,0:T(8,128)(2,1)}, bf16[4,80,2944]{2,1,0:T(8,128)(2,1)}, u32[]{:S(2)}, u32[]{:S(2)}) collective-permute-start(bf16[4,80,2944]{2,1,0:T(8,128)(2,1)} %get-tuple-element.50), channel_id=1, source_target_pairs={{0,1},{1,0},{2,3},{3,2},{4,5},{5,4},{6,7},{7,6},{8,9},{9,8},{10,11... | collective-permute-start | bytes 5652488 | tf_op jit(solution)/shard_map/ppermute | solution.py:381
  243.4 12.7 %collective-permute-start.25 = (bf16[4,80,2944]{2,1,0:T(8,128)(2,1)}, bf16[4,80,2944]{2,1,0:T(8,128)(2,1)}, u32[]{:S(2)}, u32[]{:S(2)}) collective-permute-start(bf16[4,80,2944]{2,1,0:T(8,128)(2,1)} %get-tuple-element.52), channel_id=1, source_target_pairs={{0,1},{1,0},{2,3},{3,2},{4,5},{5,4},{6,7},{7,6},{8,9},{9,8},{10,11... | collective-permute-start | bytes 5652488 | tf_op jit(solution)/shard_map/ppermute | solution.py:381
  256.1 36.2 %collective-permute-start.18 = (bf16[512,2944]{1,0:T(8,128)(2,1)}, bf16[512,2944]{1,0:T(8,128)(2,1)}, u32[]{:S(2)}, u32[]{:S(2)}) collective-permute-start(bf16[512,2944]{1,0:T(8,128)(2,1)} %get-tuple-element.45), channel_id=1, source_target_pairs={{0,16},{1,9},{2,18},{3,11},{4,20},{5,13},{6,22},{7,15},{8,24},{9,1... | collective-permute-start | bytes 9043976 | tf_op jit(solution)/shard_map/ppermute | solution.py:455
  256.1 36.2 %copy-start.3 = (bf16[512,2944]{1,0:T(8,128)(2,1)S(1)}, bf16[512,2944]{1,0:T(8,128)(2,1)}, u32[]{:S(2)}) copy-start(bf16[512,2944]{1,0:T(8,128)(2,1)} %get-tuple-element.44) | copy-start | bytes 9043972
  281.1 13.5 %collective-permute-start.26 = (bf16[4,80,2944]{2,1,0:T(8,128)(2,1)}, bf16[4,80,2944]{2,1,0:T(8,128)(2,1)}, u32[]{:S(2)}, u32[]{:S(2)}) collective-permute-start(bf16[4,80,2944]{2,1,0:T(8,128)(2,1)} %get-tuple-element.54), channel_id=1, source_target_pairs={{0,1},{1,0},{2,3},{3,2},{4,5},{5,4},{6,7},{7,6},{8,9},{9,8},{10,11... | collective-permute-start | bytes 5652488 | tf_op jit(solution)/shard_map/ppermute | solution.py:381
  281.4 19.5 %collective-permute-start.30 = (bf16[4,80,2944]{2,1,0:T(8,128)(2,1)}, bf16[4,80,2944]{2,1,0:T(8,128)(2,1)}, u32[]{:S(2)}, u32[]{:S(2)}) collective-permute-start(bf16[4,80,2944]{2,1,0:T(8,128)(2,1)} %get-tuple-element.58), channel_id=1, source_target_pairs={{0,1},{1,0},{2,3},{3,2},{4,5},{5,4},{6,7},{7,6},{8,9},{9,8},{10,11... | collective-permute-start | bytes 5652488 | tf_op jit(solution)/shard_map/ppermute | solution.py:381
  294.0 31.4 %collective-permute-start.19 = (bf16[256,2944]{1,0:T(8,128)(2,1)S(1)}, bf16[256,2944]{1,0:T(8,128)(2,1)S(1)}, u32[]{:S(2)}, u32[]{:S(2)}) collective-permute-start(bf16[256,2944]{1,0:T(8,128)(2,1)S(1)} %add_convert_fusion), channel_id=1, source_target_pairs={{0,8},{1,17},{2,10},{3,19},{4,12},{5,21},{6,14},{7,23},{8,0},{9,25... | collective-permute-start | bytes 4521992 | tf_op jit(solution)/shard_map/ppermute | solution.py:455
  300.7 35.6 %collective-permute-start.27 = (bf16[256,2944]{1,0:T(8,128)(2,1)}, bf16[256,2944]{1,0:T(8,128)(2,1)}, u32[]{:S(2)}, u32[]{:S(2)}) collective-permute-start(bf16[256,2944]{1,0:T(8,128)(2,1)} %get-tuple-element.56), channel_id=1, source_target_pairs={{0,16},{1,9},{2,18},{3,11},{4,20},{5,13},{6,22},{7,15},{8,24},{9,1... | collective-permute-start | bytes 4521992 | tf_op jit(solution)/shard_map/ppermute | solution.py:455
  332.6 33.2 %collective-permute-start.31 = (bf16[256,2944]{1,0:T(8,128)(2,1)}, bf16[256,2944]{1,0:T(8,128)(2,1)S(1)}, u32[]{:S(2)}, u32[]{:S(2)}) collective-permute-start(bf16[256,2944]{1,0:T(8,128)(2,1)} %get-tuple-element.60), channel_id=1, source_target_pairs={{0,16},{1,9},{2,18},{3,11},{4,20},{5,13},{6,22},{7,15},{8,24},{9,1... | collective-permute-start | bytes 4521992 | tf_op jit(solution)/shard_map/ppermute | solution.py:455
  336.0 29.9 %collective-permute-start.20 = (bf16[128,2944]{1,0:T(8,128)(2,1)S(1)}, bf16[128,2944]{1,0:T(8,128)(2,1)S(1)}, u32[]{:S(2)}, u32[]{:S(2)}) collective-permute-start(bf16[128,2944]{1,0:T(8,128)(2,1)S(1)} %get-tuple-element.61), channel_id=1, source_target_pairs={{0,4},{2,6},{4,0},{6,2},{1,5},{3,7},{5,1},{7,3},{8,12},{10,14},{12... | collective-permute-start | bytes 2261000 | tf_op jit(solution)/shard_map/ppermute | solution.py:381
  337.6 33.7 %collective-permute-start.28 = (bf16[128,2944]{1,0:T(8,128)(2,1)S(1)}, bf16[128,2944]{1,0:T(8,128)(2,1)S(1)}, u32[]{:S(2)}, u32[]{:S(2)}) collective-permute-start(bf16[128,2944]{1,0:T(8,128)(2,1)S(1)} %add_convert_fusion.3), channel_id=1, source_target_pairs={{0,8},{1,17},{2,10},{3,19},{4,12},{5,21},{6,14},{7,23},{8,0},{9,25... | collective-permute-start | bytes 2261000 | tf_op jit(solution)/shard_map/ppermute | solution.py:455
  369.7 11.9 %copy-start = (bf16[256,2944]{1,0:T(8,128)(2,1)S(1)}, bf16[256,2944]{1,0:T(8,128)(2,1)}, u32[]{:S(2)}) copy-start(bf16[256,2944]{1,0:T(8,128)(2,1)} %get-tuple-element.59.keep_ref) | copy-start | bytes 4521988
  369.7 11.9 %copy-start.2 = (bf16[256,2944]{1,0:T(8,128)(2,1)S(1)}, bf16[256,2944]{1,0:T(8,128)(2,1)}, u32[]{:S(2)}) copy-start(bf16[256,2944]{1,0:T(8,128)(2,1)} %copy-done.1) | copy-start | bytes 4521988
  369.7 11.8 %collective-permute-start.32 = (bf16[128,2944]{1,0:T(8,128)(2,1)}, bf16[128,2944]{1,0:T(8,128)(2,1)S(1)}, u32[]{:S(2)}, u32[]{:S(2)}) collective-permute-start(bf16[128,2944]{1,0:T(8,128)(2,1)} %turn.1), channel_id=1, source_target_pairs={{0,8},{1,17},{2,10},{3,19},{4,12},{5,21},{6,14},{7,23},{8,0},{9,25... | collective-permute-start | bytes 2261000 | tf_op jit(solution)/shard_map/ppermute | solution.py:455
  372.7 21.7 %collective-permute-start.29 = (bf16[128,2944]{1,0:T(8,128)(2,1)S(1)}, bf16[128,2944]{1,0:T(8,128)(2,1)S(1)}, u32[]{:S(2)}, u32[]{:S(2)}) collective-permute-start(bf16[128,2944]{1,0:T(8,128)(2,1)S(1)} %add_convert_fusion.2), channel_id=1, source_target_pairs={{0,6},{2,4},{4,2},{6,0},{1,7},{3,5},{5,3},{7,1},{8,14},{10,12},{12... | collective-permute-start | bytes 2261000 | tf_op jit(solution)/shard_map/ppermute | solution.py:381
  381.8 26.5 %collective-permute-start.33 = (bf16[128,2944]{1,0:T(8,128)(2,1)S(1)}, bf16[128,2944]{1,0:T(8,128)(2,1)S(1)}, u32[]{:S(2)}, u32[]{:S(2)}) collective-permute-start(bf16[128,2944]{1,0:T(8,128)(2,1)S(1)} %add_convert_fusion.1), channel_id=1, source_target_pairs={{0,2},{2,0},{4,6},{6,4},{1,3},{3,1},{5,7},{7,5},{8,10},{10,8},{12,... | collective-permute-start | bytes 2261000 | tf_op jit(solution)/shard_map/ppermute | solution.py:381
  394.4 13.9 %copy-start.10 = (bf16[128,2944]{1,0:T(8,128)(2,1)}, bf16[128,2944]{1,0:T(8,128)(2,1)S(1)}, u32[]{:S(2)}) copy-start(bf16[128,2944]{1,0:T(8,128)(2,1)S(1)} %collective-permute-done.29.refs_2_) | copy-start | bytes 2260996
  (14 other events, 20.3 us)
